TPU v7x, 32 devices: a whole 2x2x4 slice. The times are simulated.
32 devices in a mesh: beams: 2 (over y), tm: 4 (over x, core), band: 4 (over z).
Axes of the slice: x: 2, y: 2, z: 4, core: 2. Of those that a mesh axis runs over, the one named last changes fastest.
Arguments:
- signal: float32 [512, 131072], P(('beams', 'band'), 'tm'), parts along dimension 0, may hold values from -6 to 6
- tree_picks: int32 [2, 8, 256], replicated, may hold values from 0 to 63, as said below
- tree_delays: int32 [8, 256], replicated, may hold values from 0 to 4
- template_bank: float32 [2, 201, 64], replicated, may hold values from -0.75 to 0.75
- template_pick: int32 [8, 64, 2], P(('beams', 'band'), 'tm'), parts along dimension 0, may hold values from 0 to 200
Outputs:
- powers: float32 [8, 64, 2, 65536], P(('beams', 'band'), 'tm'), parts along dimension 0
There are 2 independent parts, one for each index of `beams`. A program takes and returns all parts, laid end to end along the dimension named above; an argument that names none is the same for every part. Nothing has to cross between parts.
Inputs may be any that keep to these rules, and one draw needn't show every extreme that they name: `tree_picks`: entries of section j are below the smaller of 2 to the power j and 64.
All inputs are finite; a program needn't handle non-finite values.
Results may differ from a plain program's by a relative error of at most 0.00007.
Values sent between devices are 32-bit elements; how exact they have to be, the bound alone decides.
A program may use at most 192 MiB of HBM per device.

v0:
```python
import math

import jax
import jax.numpy as jnp
from jax import lax
from jax.sharding import PartitionSpec as P

CH_DEV = 64
LOGCD = 6
MAXD = 4


radix_rows = 128


def shifted(value, axis, steps):
    count = lax.axis_size(axis)
    first, last = (max(0, -steps), min(count, count - steps))
    return lax.ppermute(value, axis, [(source, source + steps) for source in range(first, last)])


def delayed_rows(upper_rows, delays, out_len):
    total = jnp.zeros((upper_rows.shape[0], out_len), upper_rows.dtype)
    for shift_by in range(MAXD + 1):
        total = total + jnp.where(
            delays[:, None] == shift_by, upper_rows[:, shift_by : shift_by + out_len], 0.0
        )
    return total


def group_section(block, section_num, pick_low, pick_high, delays, out_len):
    row_count = block.shape[0]
    half_size = 1 << section_num
    global_row = jnp.arange(row_count, dtype=jnp.int32)
    base_row = (
        global_row
        - global_row % (2 * half_size)
        + global_row % half_size
        - global_row % min(half_size, CH_DEV)
    )
    low_rows = jnp.take(block, base_row + pick_low, axis=0)
    high_rows = jnp.take(block, base_row + half_size + pick_high, axis=0)
    return low_rows[:, :out_len] + delayed_rows(high_rows, delays, out_len)


def template_powers(spec_re, spec_im, tmpl_re, tmpl_im):
    trials, freq_count = spec_re.shape
    tap_count = tmpl_re.shape[-1]
    block_count = freq_count // 128
    highest = lax.Precision.HIGHEST

    def windows(spectrum):
        padded = jnp.pad(spectrum, ((0, 0), (tap_count // 2, 128 - tap_count // 2)))
        tiles = padded.reshape(trials, block_count + 1, 128)
        return jnp.concatenate([tiles[:, :-1], tiles[:, 1:, :tap_count]], axis=2)

    lag_matrix = (
        jnp.arange(128 + tap_count, dtype=jnp.int32)[:, None]
        - jnp.arange(128, dtype=jnp.int32)[None, :]
    )
    in_band = (lag_matrix >= 0) & (lag_matrix < tap_count)
    lag_index = jnp.clip(lag_matrix, 0, tap_count - 1)
    band_re = jnp.where(in_band, tmpl_re[..., lag_index], 0.0)
    band_im = jnp.where(in_band, tmpl_im[..., lag_index], 0.0)
    win_re = windows(spec_re)
    win_im = windows(spec_im)
    out_re = jnp.einsum("tbj,tzji->tzbi", win_re, band_re, precision=highest) - jnp.einsum(
        "tbj,tzji->tzbi", win_im, band_im, precision=highest
    )
    out_im = jnp.einsum("tbj,tzji->tzbi", win_re, band_im, precision=highest) + jnp.einsum(
        "tbj,tzji->tzbi", win_im, band_re, precision=highest
    )
    return (out_re * out_re + out_im * out_im).reshape(trials, tmpl_re.shape[1], freq_count)


def spectra(series, picks, template_bank, channels):
    trials, samples = series.shape
    highest = lax.Precision.HIGHEST
    col_count = samples // radix_rows
    half_cols = col_count // 2
    two_pi = 2.0 * math.pi
    norm_scale = 1.0 / math.sqrt(samples * channels)
    shaped = (series * norm_scale).reshape(trials, radix_rows, col_count)
    row_iota = jnp.arange(radix_rows, dtype=jnp.int32)
    col_iota = jnp.arange(col_count, dtype=jnp.int32)
    angle_rows = (row_iota[:, None] * row_iota[None, :] % radix_rows).astype(jnp.float32) * (
        two_pi / radix_rows
    )
    first_re = jnp.einsum("ac,tab->tcb", jnp.cos(angle_rows), shaped, precision=highest)
    first_im = -jnp.einsum("ac,tab->tcb", jnp.sin(angle_rows), shaped, precision=highest)
    twiddle = (row_iota[:, None] * col_iota[None, :] % samples).astype(jnp.float32) * (
        two_pi / samples
    )
    tw_cos = jnp.cos(twiddle)
    tw_sin = jnp.sin(twiddle)
    mid_re = first_re * tw_cos + first_im * tw_sin
    mid_im = first_im * tw_cos - first_re * tw_sin
    angle_cols = (col_iota[:half_cols, None] * col_iota[None, :] % col_count).astype(
        jnp.float32
    ) * (two_pi / col_count)
    cos_cols = jnp.cos(angle_cols)
    sin_cols = jnp.sin(angle_cols)
    spec_re = jnp.einsum("db,tcb->tdc", cos_cols, mid_re, precision=highest) + jnp.einsum(
        "db,tcb->tdc", sin_cols, mid_im, precision=highest
    )
    spec_im = jnp.einsum("db,tcb->tdc", cos_cols, mid_im, precision=highest) - jnp.einsum(
        "db,tcb->tdc", sin_cols, mid_re, precision=highest
    )
    spec_re = spec_re.reshape(trials, samples // 2)
    spec_im = spec_im.reshape(trials, samples // 2)
    onehot = (picks[:, :, None] == jnp.arange(template_bank.shape[1], dtype=jnp.int32)).astype(
        jnp.float32
    )
    chosen = jnp.einsum("tzk,ckm->ctzm", onehot, template_bank, precision=highest)
    return template_powers(spec_re, spec_im, chosen[0], chosen[1])


def on_device(signal, tree_picks, tree_delays, template_bank, template_pick):
    band_count = lax.axis_size("band")
    time_count = lax.axis_size("tm")
    cross_count = band_count.bit_length() - 1
    sections = LOGCD + cross_count
    rim_depth = sections * MAXD
    folded = lax.all_to_all(signal, "band", split_axis=1, concat_axis=0, tiled=True)
    slab_len = folded.shape[1]
    rim_cols = shifted(folded[:, :rim_depth], ("tm", "band"), -1)
    extended = jnp.concatenate([folded, rim_cols], axis=1)
    length = slab_len + rim_depth
    for section_num in range(sections):
        length = length - MAXD
        extended = group_section(
            extended,
            section_num,
            tree_picks[0, section_num],
            tree_picks[1, section_num],
            tree_delays[section_num],
            length,
        )
        extended = lax.optimization_barrier(extended)
    channels = extended.shape[0]
    trials = CH_DEV // time_count
    ordered = (
        extended.reshape(band_count, time_count, trials, slab_len)
        .transpose(1, 0, 2, 3)
        .reshape(channels, slab_len)
    )
    series = lax.all_to_all(ordered, ("tm", "band"), split_axis=0, concat_axis=1, tiled=True)
    powers = spectra(series, template_pick[0], template_bank, CH_DEV * band_count)
    return powers[None]


def solution(mesh):
    in_specs = (P(("beams", "band"), "tm"), P(), P(), P(), P(("beams", "band"), "tm", None))
    out_specs = P(("beams", "band"), "tm", None, None)
    return jax.shard_map(
        on_device, mesh=mesh, in_specs=in_specs, out_specs=out_specs, check_vma=False
    )
```

profile of v0, /device:TPU:0, one launch (start us, length us, event | category | flops | bytes accessed | tf_op | source)
XLA Modules:
  0.0 1344.3 jit_solution(8012996367653712904)
XLA Ops:
  27.5 170.8 %all-to-all-done = f32[64,4,8192]{2,0,1:T(8,128)} async-done(((f32[64,4,8192]{2,0,1:T(8,128)}), f32[64,4,8192]{2,0,1:T(8,128)}, u32[]{:S(2)}, u32[]{:S(2)}) %all-to-all-start) | async-done | bytes 8388640 | tf_op jit(solution)/shard_map/all_to_all | solution.py:124
  213.4 13.4 gather_fusion.3
  226.7 25.2 %gather_fusion.2 = f32[256,8224]{1,0:T(8,128)} fusion(f32[256,8224]{1,0:T(8,128)} %pad_maximum_fusion, s32[1024]{0:T(1024)S(1)} %pad_clamp_fusion.15), kind=kCustom, calls=%fused_computation.clone | custom fusion | bytes 16843776 | tf_op jit(solution)/shard_map/jit(_take)/gather | solution.py:41
  257.8 10.8 fusion.31
  268.6 13.4 gather_fusion.5
  281.9 13.8 %gather_fusion.4 = f32[256,8220]{1,0:T(8,128)} fusion(f32[256,8220]{1,0:T(8,128)} %fusion.31, s32[1024]{0:T(1024)S(1)} %pad_clamp_fusion.13), kind=kCustom, calls=%fused_computation.1.clone | custom fusion | bytes 16835584 | tf_op jit(solution)/shard_map/jit(_take)/gather | solution.py:41
  301.6 10.8 fusion.26
  312.4 13.4 gather_fusion.7
  325.8 13.7 %gather_fusion.6 = f32[256,8216]{1,0:T(8,128)} fusion(f32[256,8216]{1,0:T(8,128)} %fusion.26, s32[1024]{0:T(1024)} %pad_clamp_fusion.11), kind=kCustom, calls=%fused_computation.2.clone | custom fusion | bytes 16827392 | tf_op jit(solution)/shard_map/jit(_take)/gather | solution.py:41
  356.1 13.5 %gather_fusion.9 = f32[256,8212]{1,0:T(8,128)} fusion(f32[256,8212]{1,0:T(8,128)} %fusion.21, s32[1024]{0:T(1024)} %pad_clamp_fusion.8), kind=kCustom, calls=%fused_computation.11.clone | custom fusion | bytes 16819200 | tf_op jit(solution)/shard_map/jit(_take)/gather | solution.py:42
  369.6 13.9 %gather_fusion.8 = f32[256,8212]{1,0:T(8,128)} fusion(f32[256,8212]{1,0:T(8,128)} %fusion.21, s32[1024]{0:T(1024)} %pad_clamp_fusion.9), kind=kCustom, calls=%fused_computation.3.clone | custom fusion | bytes 16819200 | tf_op jit(solution)/shard_map/jit(_take)/gather | solution.py:41
  400.2 13.5 %gather_fusion.11 = f32[256,8208]{1,0:T(8,128)} fusion(f32[256,8208]{1,0:T(8,128)} %fusion.16, s32[1024]{0:T(1024)} %pad_clamp_fusion.6), kind=kCustom, calls=%fused_computation.12.clone | custom fusion | bytes 16811008 | tf_op jit(solution)/shard_map/jit(_take)/gather | solution.py:42
  413.7 13.7 %gather_fusion.10 = f32[256,8208]{1,0:T(8,128)} fusion(f32[256,8208]{1,0:T(8,128)} %fusion.16, s32[1024]{0:T(1024)} %pad_clamp_fusion.7), kind=kCustom, calls=%fused_computation.4.clone | custom fusion | bytes 16811008 | tf_op jit(solution)/shard_map/jit(_take)/gather | solution.py:41
  444.1 13.5 %gather_fusion.13 = f32[256,8204]{1,0:T(8,128)} fusion(f32[256,8204]{1,0:T(8,128)} %fusion.11, s32[1024]{0:T(1024)} %pad_clamp_fusion.4), kind=kCustom, calls=%fused_computation.13.clone | custom fusion | bytes 16802816 | tf_op jit(solution)/shard_map/jit(_take)/gather | solution.py:42
  457.6 13.9 %gather_fusion.12 = f32[256,8204]{1,0:T(8,128)} fusion(f32[256,8204]{1,0:T(8,128)} %fusion.11, s32[1024]{0:T(1024)} %pad_clamp_fusion.5), kind=kCustom, calls=%fused_computation.5.clone | custom fusion | bytes 16802816 | tf_op jit(solution)/shard_map/jit(_take)/gather | solution.py:41
  488.2 13.5 %gather_fusion.15 = f32[256,8200]{1,0:T(8,128)} fusion(f32[256,8200]{1,0:T(8,128)} %fusion.6, s32[1024]{0:T(1024)} %pad_clamp_fusion.2), kind=kCustom, calls=%fused_computation.14.clone | custom fusion | bytes 16794624 | tf_op jit(solution)/shard_map/jit(_take)/gather | solution.py:42
  501.7 13.7 %gather_fusion.14 = f32[256,8200]{1,0:T(8,128)} fusion(f32[256,8200]{1,0:T(8,128)} %fusion.6, s32[1024]{0:T(1024)} %pad_clamp_fusion.3), kind=kCustom, calls=%fused_computation.6.clone | custom fusion | bytes 16794624 | tf_op jit(solution)/shard_map/jit(_take)/gather | solution.py:41
  532.1 13.5 %gather_fusion.17 = f32[256,8196]{1,0:T(8,128)} fusion(f32[256,8196]{1,0:T(8,128)} %fusion.1, s32[1024]{0:T(1024)} %pad_clamp_fusion), kind=kCustom, calls=%fused_computation.15.clone | custom fusion | bytes 16786432 | tf_op jit(solution)/shard_map/jit(_take)/gather | solution.py:42
  545.6 13.9 %gather_fusion.16 = f32[256,8196]{1,0:T(8,128)} fusion(f32[256,8196]{1,0:T(8,128)} %fusion.1, s32[1024]{0:T(1024)} %pad_clamp_fusion.1), kind=kCustom, calls=%fused_computation.7.clone | custom fusion | bytes 16786432 | tf_op jit(solution)/shard_map/jit(_take)/gather | solution.py:41
  590.0 166.8 %gather_fusion.1 = f32[24576,16,2]{1,2,0:T(2,128)} fusion(f32[16,2,64]{0,1,2:T(2,128)S(1)} %copy.25, s32[24576]{0:T(1024)S(1)} %fusion.102), kind=kCustom, calls=%fused_computation.17 | custom fusion | bytes 6389760 | tf_op jit(solution)/shard_map/gather | solution.py:64
  756.8 21.1 %copy.26 = f32[192,128,16,2]{1,0,3,2:T(8,128)} copy(f32[192,128,16,2]{2,3,1,0:T(2,128)} %bitcast.144) | data formatting | bytes 6291456 | tf_op jit(solution)/shard_map/gather | solution.py:64
  778.0 166.8 %gather_fusion = f32[24576,16,2]{1,2,0:T(2,128)} fusion(f32[16,2,64]{0,1,2:T(2,128)S(1)} %copy.13, s32[24576]{0:T(1024)S(1)} %fusion.102), kind=kCustom, calls=%fused_computation.16 | custom fusion | bytes 6389760 | tf_op jit(solution)/shard_map/gather | solution.py:63
  944.7 21.1 %copy.14 = f32[192,128,16,2]{1,0,3,2:T(8,128)} copy(f32[192,128,16,2]{2,3,1,0:T(2,128)} %bitcast.143) | data formatting | bytes 6291456 | tf_op jit(solution)/shard_map/gather | solution.py:63
  989.7 16.5 %fusion.111 = f32[16,1024,128]{2,1,0:T(8,128)S(1)} fusion(f32[16,128,1024]{2,1,0:T(8,128)} %mul.183), kind=kOutput, calls=%fused_computation.197 | convolution fusion | flops 3221454848 | bytes 16777216 | tf_op jit(solution)/shard_map/ac,tab->tcb/dot_general | solution.py:89
  1006.3 13.4 fusion.109
  1019.7 49.8 %fusion.61 = f32[16,128,512]{2,1,0:T(8,128)} fusion(f32[16,1024,128]{2,1,0:T(8,128)S(1)} %fusion.111, f32[16,1024,128]{2,1,0:T(8,128)S(1)} %fusion.109, f32[128,1024]{0,1:T(8,128)S(1)} %get-tuple-element.124, f32[128,1024]{0,1:T(8,128)S(1)} %get-tuple-element.125, s32[512]{0:T(512)S(1)} %slice.320), kind=kOutput, calls=%fused_computation.150 | convolution fusion | flops 12900630528 | bytes 22022144 | tf_op jit(solution)/shard_map/db,tcb->tdc/dot_general | solution.py:103
  1069.5 39.0 %add_bitcast_fusion.1 = f32[16,512,128]{1,2,0:T(8,128)} fusion(f32[16,128,512]{2,1,0:T(8,128)} %fusion.61, f32[16,1024,128]{2,1,0:T(8,128)S(1)} %fusion.111, f32[16,1024,128]{2,1,0:T(8,128)S(1)} %fusion.109, f32[128,1024]{0,1:T(8,128)S(1)} %get-tuple-element.124, f32[128,1024]{0,1:T(8,128)S(1)} %get-tuple-element.125, s32[512]{0:T(512)S(1)} %slice.320), kind=kOutput, calls=%fused_computation.133 | convolution fusion | flops 12901679104 | bytes 26216448 | tf_op jit(solution)/shard_map/db,tcb->tdc/dot_general | solution.py:103
  1135.1 40.9 %fusion.59 = f32[16,128,512]{2,1,0:T(8,128)} fusion(f32[16,1024,128]{2,1,0:T(8,128)S(1)} %bitcast.137, f32[16,1024,128]{2,1,0:T(8,128)} %copy-done.3, f32[128,1024]{0,1:T(8,128)S(1)} %get-tuple-element.124, f32[128,1024]{0,1:T(8,128)S(1)} %get-tuple-element.125, s32[512]{0:T(512)S(1)} %slice.320), kind=kOutput, calls=%fused_computation.148 | convolution fusion | flops 12900630528 | bytes 22022144 | tf_op jit(solution)/shard_map/db,tcb->tdc/dot_general | solution.py:106
  1175.9 51.6 %subtract_bitcast_fusion = f32[16,512,128]{1,2,0:T(8,128)} fusion(f32[16,128,512]{2,1,0:T(8,128)} %fusion.59, f32[16,1024,128]{2,1,0:T(8,128)S(1)} %bitcast.137, f32[16,1024,128]{2,1,0:T(8,128)S(1)} %bitcast.139, f32[128,1024]{0,1:T(8,128)S(1)} %get-tuple-element.124, f32[128,1024]{0,1:T(8,128)S(1)} %get-tuple-element.125, s32[512]{0:T(512)S(1)} %slice.320), kind=kOutput, calls=%fused_computation.132 | convolution fusion | flops 12901679104 | bytes 26216448 | tf_op jit(solution)/shard_map/db,tcb->tdc/dot_general | solution.py:106
  1270.1 11.9 fusion.42
  1301.4 19.5 %add_bitcast_fusion = f32[16,2,512,128]{2,3,1,0:T(8,128)} fusion(f32[16,2,128,512]{3,2,1,0:T(8,128)} %fusion.44, f32[16,2,128,512]{3,2,1,0:T(8,128)} %fusion.42, f32[16,2,128,512]{3,2,1,0:T(8,128)} %fusion.43, f32[16,512,64]{1,2,0:T(8,128)} %copy.46, f32[16,512,128]{1,2,0:T(8,128)} %copy.45, f32[192,128,16,2]{1,0,3,2:T(8,128)S(1)} %copy-done.16, ...), kind=kOutput, calls=%fused_computation.114 | convolution fusion | flops 4844683264 | bytes 43016192 | tf_op jit(solution)/shard_map/tbj,tzji->tzbi/dot_general | solution.py:67
  1330.1 14.0 %reshape.700 = f32[1,16,2,65536]{3,2,1,0:T(2,128)} reshape(f32[16,2,512,128]{3,2,1,0:T(8,128)} %copy.43) | data formatting | bytes 16777216 | tf_op jit(solution)/shard_map/broadcast_in_dim;reshape | solution.py:149
  (226 shorter events, 289.1 us)
Async XLA Ops:
  0.0 589.6 %copy-start = (f32[2,201,64]{1,2,0:T(8,128)S(1)}, f32[2,201,64]{1,2,0:T(8,128)}, u32[]{:S(2)}) copy-start(f32[2,201,64]{1,2,0:T(8,128)} %param.24) | copy-start | bytes 308740
  7.7 6.5 copy-start.19
  7.7 18.5 %copy-start.20 = (s32[8,256]{1,0:T(8,128)S(1)}, s32[8,256]{1,0:T(8,128)}, u32[]{:S(2)}) copy-start(s32[8,256]{1,0:T(8,128)} %param.23) | copy-start | bytes 24580
  7.7 190.5 %all-to-all-start = ((f32[64,4,8192]{2,0,1:T(8,128)}), f32[64,4,8192]{2,0,1:T(8,128)}, u32[]{:S(2)}, u32[]{:S(2)}) async-start(f32[64,4,8192]{2,0,1:T(8,128)} %bitcast.141), calls=%async_computation | async-start | bytes 16777216 | tf_op jit(solution)/shard_map/all_to_all | solution.py:124
  199.2 6.9 collective-permute-start
  325.8 13.7 %copy-start.62 = (pred[256]{0:T(512)(128)(4,1)S(1)}, pred[256]{0:T(512)(128)(4,1)}, u32[]{:S(2)}) copy-start(pred[256]{0:T(512)(128)(4,1)} %get-tuple-element.75) | copy-start | bytes 772
  339.5 5.8 copy-start.46
  339.5 5.8 copy-start.47
  369.6 13.9 %copy-start.61 = (pred[256]{0:T(512)(128)(4,1)S(1)}, pred[256]{0:T(512)(128)(4,1)}, u32[]{:S(2)}) copy-start(pred[256]{0:T(512)(128)(4,1)} %get-tuple-element.71) | copy-start | bytes 772
  383.6 5.8 copy-start.42
  413.7 13.7 %copy-start.60 = (pred[256]{0:T(512)(128)(4,1)S(1)}, pred[256]{0:T(512)(128)(4,1)}, u32[]{:S(2)}) copy-start(pred[256]{0:T(512)(128)(4,1)} %get-tuple-element.67) | copy-start | bytes 772
  427.4 5.8 copy-start.37
  457.6 13.9 %copy-start.59 = (pred[256]{0:T(512)(128)(4,1)S(1)}, pred[256]{0:T(512)(128)(4,1)}, u32[]{:S(2)}) copy-start(pred[256]{0:T(512)(128)(4,1)} %get-tuple-element.63) | copy-start | bytes 772
  471.5 5.8 copy-start.32
  501.7 13.7 %copy-start.58 = (pred[256]{0:T(512)(128)(4,1)S(1)}, pred[256]{0:T(512)(128)(4,1)}, u32[]{:S(2)}) copy-start(pred[256]{0:T(512)(128)(4,1)} %get-tuple-element.59) | copy-start | bytes 772
  515.4 5.8 copy-start.27
  545.6 13.9 %copy-start.57 = (pred[256]{0:T(512)(128)(4,1)S(1)}, pred[256]{0:T(512)(128)(4,1)}, u32[]{:S(2)}) copy-start(pred[256]{0:T(512)(128)(4,1)} %get-tuple-element.55) | copy-start | bytes 772
  559.5 5.8 copy-start.22
  583.6 5.9 copy-start.63
  583.6 384.3 %all-to-all-start.1 = ((f32[16,16,8192]{2,1,0:T(8,128)}), f32[16,16,8192]{2,1,0:T(8,128)}, u32[]{:S(2)}, u32[]{:S(2)}) async-start(f32[16,16,8192]{2,1,0:T(8,128)} %bitcast.142), calls=%async_computation.1 | async-start | bytes 16777216 | tf_op jit(solution)/shard_map/all_to_all | solution.py:147
  989.7 16.5 %copy-start.1 = (f32[16,128,1024]{2,1,0:T(8,128)S(1)}, f32[16,128,1024]{2,1,0:T(8,128)}, u32[]{:S(2)}) copy-start(f32[16,128,1024]{2,1,0:T(8,128)} %mul.183) | copy-start | bytes 25165828
  1006.3 63.2 %copy-start.2 = (f32[16,1024,128]{2,1,0:T(8,128)}, f32[16,1024,128]{2,1,0:T(8,128)S(1)}, u32[]{:S(2)}) copy-start(f32[16,1024,128]{2,1,0:T(8,128)S(1)} %fusion.111) | copy-start | bytes 25165828
  1019.7 49.9 %copy-start.3 = (f32[16,1024,128]{2,1,0:T(8,128)}, f32[16,1024,128]{2,1,0:T(8,128)S(1)}, u32[]{:S(2)}) copy-start(f32[16,1024,128]{2,1,0:T(8,128)S(1)} %fusion.109) | copy-start | bytes 25165828
  1125.4 9.6 slice-start
  1130.2 45.7 %slice-start.2 = ((s8[8388608]{0:T(1024)(128)(4,1)}), s8[4194304]{0:T(1024)(128)(4,1)S(1)}, s32[]{:S(2)}) async-start(s8[8388608]{0:T(1024)(128)(4,1)} %bitcast.138), calls=%async_computation.4 | async-start | bytes 8388608
  1135.1 40.9 %slice-start.3 = ((s8[8388608]{0:T(1024)(128)(4,1)}), s8[4194304]{0:T(1024)(128)(4,1)S(1)}, s32[]{:S(2)}) async-start(s8[8388608]{0:T(1024)(128)(4,1)} %bitcast.138), calls=%async_computation.5 | async-start | bytes 8388608
  1260.8 9.3 copy-start.16
  1270.0 11.9 copy-start.4
  1270.0 12.0 copy-start.15
  1270.1 11.9 copy-start.18
  1282.0 9.8 copy-start.5
  1282.0 9.8 copy-start.17
  (39 other events, 225.6 us)
where the time goes:
time: 1360 us; the launch traced here: 1340 us
  local copies, waits for them, and re-layouts  744 us (55%)
  matrix products  262 us (19%)
  waiting for transfers between devices  176 us (13%)
  other arithmetic  148 us (11%)
  starting transfers between devices  13.6 us (1%)
    gather x2, local copies, waits for them, and re-layouts, template_powers(): band_im = jnp.where(in_band, tmpl_im[..., lag_index], 0.0)  188 us
    gather x2, local copies, waits for them, and re-layouts, template_powers(): band_re = jnp.where(in_band, tmpl_re[..., lag_index], 0.0)  188 us
    all_to_all x1, waiting for transfers between devices, on_device(): lax.all_to_all(signal, 'band', split_axis=1, concat_axis=0, tiled=True)  171 us
    gather x8, local copies, waits for them, and re-layouts, group_section(): low_rows = jnp.take(block, base_row + pick_low, axis=0)  122 us
    gather x8, local copies, waits for them, and re-layouts, group_section(): high_rows = jnp.take(block, base_row + half_size + pick_high, axis=0)  108 us
    add x8, other arithmetic, group_section(): return low_rows[:, :out_len] + delayed_rows(high_rows, delays, out_len)  86.3 us
    dot_general x1, matrix products, spectra(): jnp.einsum('db,tcb->tdc', cos_cols, mid_im, precision=highest)  51.6 us
    dot_general x1, matrix products, spectra(): jnp.einsum('db,tcb->tdc', sin_cols, mid_im, precision=highest)  49.8 us
  transfers between devices with their start and end apart: 3, of which 2 were waited for; matrix products, arithmetic and copies ran while one was open for 29% of the time, Pallas kernels for 0%

commit v1 on v0

v1 whole, which is shorter than its diff:
```python
import functools
import math

import jax
import jax.numpy as jnp
import ml_dtypes
import numpy as np
from jax import lax
from jax.experimental import pallas as pl
from jax.experimental.pallas import tpu as pltpu
from jax.sharding import PartitionSpec as P

CH_DEV = 64
LOGCD = 6
MAXD = 4
LANES = 128
SUBS = 8
RADIX = 256
LIMIT = 56 * 1024 * 1024


def shifted(value, axis, steps):
    count = lax.axis_size(axis)
    first, last = (max(0, -steps), min(count, count - steps))
    return lax.ppermute(value, axis, [(source, source + steps) for source in range(first, last)])


def tree_kernel(sections, chunks, low_ref, high_ref, delay_ref, row_ref, x_ref, rim_ref, *rest):
    outs, (buf_a, buf_b) = rest[:chunks], rest[chunks:]
    rows, _, width = x_ref.shape
    tiles = width // LANES
    per = rows // chunks
    lane = lax.broadcasted_iota(jnp.int32, (SUBS, LANES), 1)
    sub = lax.broadcasted_iota(jnp.int32, (SUBS, LANES), 0)

    @pl.loop(0, rows, unroll=4)
    def _(r):
        head = x_ref[r, :, 0:LANES]
        buf_a[r, :, 0:width] = x_ref[r]
        up = pltpu.roll(head, SUBS - 1, 0)
        buf_a[r, :, width : width + LANES] = jnp.where(sub == SUBS - 1, rim_ref[r], up)

    def merge(src, section, r, dst, at, count):
        a = low_ref[section, r]
        b = high_ref[section, r]
        d = delay_ref[section, r]
        turn = lax.rem(LANES - d, LANES)
        keep = lane < LANES - d
        turned = [
            pltpu.roll(src[b, :, i * LANES : (i + 1) * LANES], turn, 1) for i in range(tiles + 1)
        ]
        for i in range(count):
            later = turned[min(i + 1, tiles)]
            dst[at, :, i * LANES : (i + 1) * LANES] = src[
                a, :, i * LANES : (i + 1) * LANES
            ] + jnp.where(keep, turned[i], later)

    src, dst = buf_a, buf_b
    for section in range(sections - 1):

        @pl.loop(0, rows, unroll=4)
        def _(r, src=src, dst=dst, section=section):
            merge(src, section, r, dst, r, tiles + 1)

        src, dst = dst, src
    for q in range(chunks):

        @pl.loop(0, per, unroll=4)
        def _(i, q=q, src=src):
            merge(src, sections - 1, row_ref[q, i], outs[q], i, tiles)


def tree(x, rim, low, high, delays, order):
    rows, _, width = x.shape
    chunks, per = order.shape
    sections = low.shape[0]
    smem = pl.BlockSpec(memory_space=pltpu.SMEM)
    vmem = pl.BlockSpec(memory_space=pltpu.VMEM)
    return pl.pallas_call(
        functools.partial(tree_kernel, sections, chunks),
        out_shape=[jax.ShapeDtypeStruct((per, SUBS, width), jnp.float32)] * chunks,
        in_specs=[smem] * 4 + [vmem] * 2,
        out_specs=[vmem] * chunks,
        scratch_shapes=[pltpu.VMEM((rows, SUBS, width + LANES), jnp.float32)] * 2,
        compiler_params=pltpu.CompilerParams(vmem_limit_bytes=LIMIT),
        cost_estimate=pl.CostEstimate(
            flops=rows * SUBS * width * sections * 4,
            bytes_accessed=rows * SUBS * width * 8,
            transcendentals=0,
        ),
        name="tree",
    )(low, high, delays, order, x, rim)


def split(value):
    high = value.astype(jnp.bfloat16)
    return high, (value - high.astype(jnp.float32)).astype(jnp.bfloat16)


def bands_kernel(zsel, u_ref, high_ref, low_ref):
    for z in range(zsel):
        pair = []
        for part in range(2):
            row = u_ref[0, 2 * z + part : 2 * z + part + 1, :]
            wide = jnp.broadcast_to(row, (RADIX, RADIX))
            band = pltpu.roll(wide, 0, 1, stride=1, stride_axis=0)[:, :LANES]
            pair.append(split(band))
        at = 2 * z * LANES
        for ref, real, imag in (
            (high_ref, pair[0][0], pair[1][0]),
            (low_ref, pair[0][1], pair[1][1]),
        ):
            ref[0, :RADIX, at : at + LANES] = real
            ref[0, RADIX:, at : at + LANES] = -imag
            ref[0, :RADIX, at + LANES : at + 2 * LANES] = imag
            ref[0, RADIX:, at + LANES : at + 2 * LANES] = real


def bands(picks, template_bank):
    trials, zsel = picks.shape
    taps = template_bank.shape[2]
    onehot = (picks[:, :, None] == jnp.arange(template_bank.shape[1], dtype=jnp.int32)).astype(
        jnp.float32
    )
    reversed_bank = jnp.concatenate(
        [
            template_bank[:, :, :1],
            jnp.zeros(template_bank.shape[:2] + (RADIX - taps,), jnp.float32),
            template_bank[:, :, :0:-1],
        ],
        axis=2,
    )
    u = jnp.einsum("tzk,ckm->tzcm", onehot, reversed_bank, precision=lax.Precision.HIGHEST)
    u = u.reshape(trials, 2 * zsel, RADIX)
    wide = 2 * zsel * LANES
    shape = jax.ShapeDtypeStruct((trials, 2 * RADIX, wide), jnp.bfloat16)
    spec = pl.BlockSpec((1, 2 * RADIX, wide), lambda t: (t, 0, 0))
    return pl.pallas_call(
        functools.partial(bands_kernel, zsel),
        grid=(trials,),
        out_shape=[shape, shape],
        in_specs=[pl.BlockSpec((1, 2 * zsel, RADIX), lambda t: (t, 0, 0))],
        out_specs=[spec, spec],
        compiler_params=pltpu.CompilerParams(vmem_limit_bytes=LIMIT),
        cost_estimate=pl.CostEstimate(
            flops=trials * RADIX * RADIX * 20,
            bytes_accessed=trials * 2 * RADIX * wide * 4,
            transcendentals=0,
        ),
        name="bands",
    )(u)


def tables(samples, channels, width, taps):
    cols = samples // RADIX
    outs = cols // 2
    split_by = width // cols if width % cols == 0 else 1
    place = np.arange(RADIX)
    row_of = split_by * (place % (RADIX // split_by)) + place // (RADIX // split_by)
    freq = (np.arange(RADIX) - taps // 2) % RADIX
    b = np.arange(cols)
    scale = 1.0 / math.sqrt(samples * channels)
    angle = 2.0 * np.pi / RADIX * (row_of[:, None] * freq[None, :] % RADIX)
    first = np.concatenate([np.cos(angle), -np.sin(angle)], axis=1) * scale
    angle = 2.0 * np.pi / samples * (b[:, None] * freq[None, :] % samples)
    tw_cos, tw_sin = np.cos(angle), np.sin(angle)
    angle = 2.0 * np.pi / cols * (np.arange(outs)[:, None] * b[None, :] % cols)
    second = np.concatenate([np.cos(angle), np.sin(angle)], axis=1)

    def parts(value):
        value = value.astype(np.float32)
        high = value.astype(ml_dtypes.bfloat16)
        return high, (value - high.astype(np.float32)).astype(ml_dtypes.bfloat16)

    return (
        *parts(first),
        tw_cos.astype(np.float32),
        tw_sin.astype(np.float32),
        *parts(second),
    )


def dot3(a_high, a_low, b_high, b_low):
    def dot(a, b):
        return jnp.dot(a, b, preferred_element_type=jnp.float32)

    return dot(a_high, b_high) + (dot(a_high, b_low) + dot(a_low, b_high))


def spectra_kernel(zsel, half_taps, aliased, *refs):
    x_ref, bh_ref, bl_ref, fh, fl, tc, ts, sh, sl = refs[:9]
    out_ref = refs[10] if aliased else refs[9]
    cols = tc.shape[0]
    outs = cols // 2
    x = x_ref[...]
    x = x.reshape(-1, x.shape[-1])
    if x.shape[1] != cols:
        x = jnp.concatenate(
            [x[:, i * cols : (i + 1) * cols] for i in range(x.shape[1] // cols)], axis=0
        )
    x_high, x_low = split(x.T)
    first = dot3(x_high, x_low, fh[...], fl[...])
    re, im = first[:, :RADIX], first[:, RADIX:]
    mid_re = re * tc[...] + im * ts[...]
    mid_im = im * tc[...] - re * ts[...]
    re_high, re_low = split(mid_re)
    im_high, im_low = split(mid_im)

    def block(a, b):
        return jnp.concatenate(
            [jnp.concatenate([a, b], axis=1), jnp.concatenate([b, -a], axis=1)], axis=0
        )

    spec = dot3(sh[...], sl[...], block(re_high, im_high), block(re_low, im_low))
    row = lax.broadcasted_iota(jnp.int32, (outs, RADIX), 0)
    lane = lax.broadcasted_iota(jnp.int32, (outs, RADIX), 1)
    even, odd = [], []
    for part in (spec[:, :RADIX], spec[:, RADIX:]):
        down = jnp.where(row == 0, 0.0, pltpu.roll(part, 1, 0))
        up = jnp.where(row == outs - 1, 0.0, pltpu.roll(part, outs - 1, 0))
        here = jnp.where(lane < half_taps, down, part)
        after = jnp.where(lane < half_taps, part, up)
        even.append(here)
        odd += [here[:, LANES:], after[:, :LANES]]
    window = jnp.concatenate(
        [jnp.concatenate(even, axis=1), jnp.concatenate(odd, axis=1)], axis=0
    )
    w_high, w_low = split(window)
    got = dot3(w_high, w_low, bh_ref[0], bl_ref[0])
    for z in range(zsel):
        at = 2 * z * LANES
        real, imag = got[:, at : at + LANES], got[:, at + LANES : at + 2 * LANES]
        power = real * real + imag * imag
        for e in range(2):
            out_ref[0, pl.ds(e * zsel + z, outs, 2 * zsel), :] = power[e * outs : (e + 1) * outs]


def spectra(x, band_high, band_low, consts, zsel, taps, trials, first_trial, so_far):
    cols = consts[2].shape[0]
    outs = cols // 2
    rows = 2 * outs * zsel
    if x.shape[-1] % cols == 0:
        here = x.shape[1]
        x_spec = pl.BlockSpec((x.shape[0], 1, SUBS, x.shape[-1]), lambda t: (0, t, 0, 0))
    else:
        here = x.shape[1]
        x = x.transpose(1, 0, 2, 3).reshape(here, RADIX, cols)
        x_spec = pl.BlockSpec((1, RADIX, cols), lambda t: (t, 0, 0))
    band_spec = pl.BlockSpec(
        (1,) + band_high.shape[1:], lambda t: (first_trial + t, 0, 0)
    )
    whole = [pl.BlockSpec(c.shape, lambda t: (0, 0)) for c in consts]
    aliased = so_far is not None
    more = [so_far] if aliased else []
    macs = here * (cols * RADIX * 2 * RADIX + outs * 2 * cols * 2 * RADIX + 2 * outs * 4 * RADIX * RADIX)
    return pl.pallas_call(
        functools.partial(spectra_kernel, zsel, taps // 2, aliased),
        grid=(here,),
        out_shape=jax.ShapeDtypeStruct((trials, rows, LANES), jnp.float32),
        in_specs=[x_spec, band_spec, band_spec, *whole]
        + [pl.BlockSpec(memory_space=pl.ANY)] * len(more),
        out_specs=pl.BlockSpec((1, rows, LANES), lambda t: (first_trial + t, 0, 0)),
        input_output_aliases={9: 0} if aliased else {},
        compiler_params=pltpu.CompilerParams(vmem_limit_bytes=LIMIT),
        cost_estimate=pl.CostEstimate(
            flops=6 * macs, bytes_accessed=here * 2 * 1024 * 1024, transcendentals=0
        ),
        name="spectra",
    )(x, band_high, band_low, *consts, *more)


def on_device(signal, tree_picks, tree_delays, template_bank, template_pick):
    band_count = lax.axis_size("band")
    time_count = lax.axis_size("tm")
    everyone = band_count * time_count
    sections = LOGCD + band_count.bit_length() - 1
    rim_depth = sections * MAXD
    channels = CH_DEV * band_count
    samples = signal.shape[1] * time_count
    slab = signal.shape[1] // band_count
    width = slab // SUBS
    trials = CH_DEV // time_count
    chunks = min(4, trials)
    zsel = template_pick.shape[2]
    taps = template_bank.shape[2]

    band_high, band_low = bands(template_pick[0], template_bank)

    folded = signal.reshape(CH_DEV, band_count, SUBS, width).transpose(1, 0, 2, 3)
    x = lax.all_to_all(folded, "band", split_axis=0, concat_axis=0, tiled=True)
    x = x.reshape(channels, SUBS, width)
    rim = shifted(x[:, 0, :rim_depth], ("tm", "band"), -1)
    rim = jnp.pad(rim, ((0, 0), (0, LANES - rim_depth)))
    rim = jnp.broadcast_to(rim[:, None, :], (channels, SUBS, LANES))

    half = (1 << np.arange(sections))[:, None]
    r = np.arange(channels)[None, :]
    base = r - r % (2 * half) + r % half - r % np.minimum(half, CH_DEV)
    low = tree_picks[0] + base.astype(np.int32)
    high = tree_picks[1] + (base + half).astype(np.int32)
    order = np.arange(channels).reshape(band_count, time_count, chunks, trials // chunks)
    order = order.transpose(2, 1, 0, 3).reshape(chunks, -1).astype(np.int32)
    pieces = tree(x, rim, low, high, tree_delays, jnp.asarray(order))

    consts = [jnp.asarray(c) for c in tables(samples, channels, width, taps)]
    out = None
    size = trials // chunks
    for q, piece in enumerate(pieces):
        piece = piece.reshape(everyone, size, SUBS, width)
        piece = lax.all_to_all(piece, ("tm", "band"), split_axis=0, concat_axis=0, tiled=True)
        out = spectra(piece, band_high, band_low, consts, zsel, taps, trials, q * size, out)
    out = out.reshape(trials, samples // 2 // LANES, zsel, LANES).transpose(0, 2, 1, 3)
    return out.reshape(1, trials, zsel, samples // 2)


def solution(mesh):
    in_specs = (P(("beams", "band"), "tm"), P(), P(), P(), P(("beams", "band"), "tm", None))
    out_specs = P(("beams", "band"), "tm", None, None)
    return jax.shard_map(
        on_device, mesh=mesh, in_specs=in_specs, out_specs=out_specs, check_vma=False
    )
```

time: 1360 us -> 509 us (0.37); the launches traced: 1340 us -> 508 us
  local copies, waits for them, and re-layouts: 744 us -> 17.4 us
  blocking collectives: 0 us -> 352 us
  matrix products: 262 us -> 0.33 us
  waiting for transfers between devices: 176 us -> 4.93 us
  other arithmetic: 148 us -> 0.61 us
  Pallas kernels: 0 us -> 127 us
    gather x20 -> x0, local copies, waits for them, and re-layouts: 605 us -> none  [the longest x2 188 us: template_powers(): band_im = jnp.where(in_band, tmpl_im[..., lag_index], 0.0)]
    all_to_all x0 -> x4, blocking collectives: none -> 352 us  [the longest x1 189 us: on_device(): x = lax.all_to_all(folded, 'band', split_axis=0, concat_axis=0, tiled=True)]
    dot_general x11 -> x1, matrix products: 262 us -> 0.33 us  [bands(): jnp.einsum('tzk,ckm->tzcm', onehot, reversed_bank, precision=lax.Precisio...]
    all_to_all x2 -> x1, waiting for transfers between devices: 171 us -> 0.01 us  [on_device(): lax.all_to_all(piece, ('tm', 'band'), split_axis=0, concat_axis=0, tiled=...]
    pallas_call x0 -> x6, Pallas kernels: none -> 127 us  [the longest x1 63.3 us: tree(): pl.pallas_call(functools.partial(tree_kernel, sections, chunks), out_shap...]
    add x8 -> x1, other arithmetic: 86.3 us -> 0.61 us  [on_device(): high = tree_picks[1] + (base + half).astype(np.int32)]
    select_n x8 -> x0, other arithmetic: 34.2 us -> none  [group_section(): high_rows = jnp.take(block, base_row + half_size + pick_high, axis=0)]
    unnamed x142 -> x18, local copies, waits for them, and re-layouts: 40.1 us -> 13 us
  transfers between devices with their start and end apart: 3 -> 2, of which waited for: 2 -> 1; matrix products, arithmetic and copies ran while one was open for 29% -> 1% of each run, Pallas kernels for 0% -> 10%
where the time goes in v1:
time: 509 us; the launch traced here: 508 us
  blocking collectives  352 us (69%)
  Pallas kernels  127 us (25%)
  local copies, waits for them, and re-layouts  17.4 us (3%)
  starting transfers between devices  5.19 us (1%)
    all_to_all x1, blocking collectives, on_device(): x = lax.all_to_all(folded, 'band', split_axis=0, concat_axis=0, tiled=True)  189 us
    all_to_all x3, blocking collectives, on_device(): lax.all_to_all(piece, ('tm', 'band'), split_axis=0, concat_axis=0, tiled=...  163 us
    pallas_call x1, Pallas kernels, tree(): pl.pallas_call(functools.partial(tree_kernel, sections, chunks), out_shap...  63.3 us
    pallas_call x4, Pallas kernels, spectra(): pl.pallas_call(functools.partial(spectra_kernel, zsel, taps // 2, aliased...  52.8 us
    unnamed x18, local copies, waits for them, and re-layouts  13 us
    pallas_call x1, Pallas kernels, bands(): pl.pallas_call(functools.partial(bands_kernel, zsel), grid=(trials,), out...  11.2 us
  transfers between devices with their start and end apart: 2, of which 1 were waited for; matrix products, arithmetic and copies ran while one was open for 1% of the time, Pallas kernels for 10%

profile of v1, /device:TPU:0, one launch (start us, length us, event | category | flops | bytes accessed | tf_op | source)
XLA Modules:
  0.0 508.0 jit_solution(4072816388361259271)
XLA Ops:
  0.0 8.1 %copy.26 = f32[8,8,32,1024]{3,2,1,0:T(8,128)S(1)} copy(f32[8,8,32,1024]{3,1,2,0:T(8,128)} %bitcast.35) | data formatting | bytes 16777216
  8.1 1.7 copy.28
  9.8 0.0 copy-start.4
  9.8 0.0 copy-start.5
  9.8 0.0 copy-start.6
  9.8 189.3 %all_to_all.25 = f32[4,64,8,1024]{3,2,1,0:T(8,128)S(1)} all-to-all(f32[4,64,8,1024]{3,2,1,0:T(8,128)S(1)} %bitcast.33), channel_id=1, replica_groups=mesh['beams'=2,'tm'=4,'band'=4] {'band'}, dimensions={0} | all-to-all | bytes 16777216 | tf_op jit(solution)/shard_map/all_to_all | solution.py:290
  199.1 3.4 copy-done
  202.5 0.1 slice.20
  202.6 1.3 collective-permute-start
  203.9 0.0 copy-done.4
  204.0 0.6 add_bitcast_fusion
  204.6 4.9 collective-permute-done
  209.5 1.1 broadcast_in_dim.4.rim_ref
  210.6 63.3 %tree.1 = (f32[64,8,1024]{2,1,0:T(8,128)}, f32[64,8,1024]{2,1,0:T(8,128)}, f32[64,8,1024]{2,1,0:T(8,128)}, f32[64,8,1024]{2,1,0:T(8,128)}) custom-call(s32[8,256]{1,0:T(8,128)} %get-tuple-element.18.low_ref, s32[8,256]{1,0:T(8,128)} %get-tuple-element.17.high_ref, s32[8,256]{1,0:T(8,128)} %delay_ref.1, s32[4,64]{1,0:T(4,128)} %constant.24.clone.row_ref, ...), custom_call_target="tpu_custom_call" | custom-call | flops 67108864 | bytes 16777216 | tf_op jit(solution)/shard_map/tree/pallas_call | solution.py:79
  273.9 56.1 %all_to_all.26.refs_0_ = f32[16,4,8,1024]{3,2,1,0:T(8,128)} all-to-all(f32[16,4,8,1024]{3,2,1,0:T(8,128)} %bitcast.39), channel_id=1, replica_groups=mesh['beams'=2,'tm'=4,'band'=4] {'tm','band'}, dimensions={0} | all-to-all | bytes 4194304 | tf_op jit(solution)/shard_map/all_to_all | solution.py:310
  330.1 53.8 %all_to_all.27.refs_0_ = f32[16,4,8,1024]{3,2,1,0:T(8,128)} all-to-all(f32[16,4,8,1024]{3,2,1,0:T(8,128)} %bitcast.38), channel_id=1, replica_groups=mesh['beams'=2,'tm'=4,'band'=4] {'tm','band'}, dimensions={0} | all-to-all | bytes 4194304 | tf_op jit(solution)/shard_map/all_to_all | solution.py:310
  383.9 52.7 %all_to_all.28.refs_0_ = f32[16,4,8,1024]{3,2,1,0:T(8,128)} all-to-all(f32[16,4,8,1024]{3,2,1,0:T(8,128)S(1)} %bitcast.37), channel_id=1, replica_groups=mesh['beams'=2,'tm'=4,'band'=4] {'tm','band'}, dimensions={0} | all-to-all | bytes 4194304 | tf_op jit(solution)/shard_map/all_to_all | solution.py:310
  436.6 3.9 all-to-all-start.1
  440.6 0.1 copy.25
  440.7 0.7 rev.3
  441.4 0.1 copy.20
  441.6 0.1 pad.6.clone
  441.6 0.0 copy-done.7
  441.6 0.3 fusion
  442.0 0.7 copy.24.u_ref
  442.6 11.2 %bands.1 = (bf16[16,512,512]{2,1,0:T(8,128)(2,1)}, bf16[16,512,512]{2,1,0:T(8,128)(2,1)}) custom-call(f32[16,4,256]{2,1,0:T(4,128)} %copy.24.u_ref), custom_call_target="tpu_custom_call" | custom-call | flops 20971520 | bytes 16777216 | tf_op jit(solution)/shard_map/bands/pallas_call | solution.py:138
  453.9 13.2 %spectra.4.refs_9_ = f32[16,1024,128]{2,1,0:T(8,128)} custom-call(f32[16,4,8,1024]{3,2,1,0:T(8,128)} %all_to_all.28.refs_0_, bf16[16,512,512]{2,1,0:T(8,128)(2,1)} %get-tuple-element.12.refs_1_, bf16[16,512,512]{2,1,0:T(8,128)(2,1)} %get-tuple-element.13.refs_2_, bf16[256,512]{1,0:T(8,128)(2,1)} %constant.25.clone.refs_3_, ...), custom_call_target="tpu_custom_call" | custom-call | flops 8053063680 | bytes 8388608 | tf_op jit(solution)/shard_map/spectra/pallas_call | solution.py:256
  467.1 13.2 %spectra.5.refs_9_ = f32[16,1024,128]{2,1,0:T(8,128)} custom-call(f32[16,4,8,1024]{3,2,1,0:T(8,128)} %all_to_all.27.refs_0_, bf16[16,512,512]{2,1,0:T(8,128)(2,1)} %get-tuple-element.12.refs_1_, bf16[16,512,512]{2,1,0:T(8,128)(2,1)} %get-tuple-element.13.refs_2_, bf16[256,512]{1,0:T(8,128)(2,1)} %constant.25.clone.refs_3_, ...), custom_call_target="tpu_custom_call", output_to_operand_aliasing={{}: (9, {})} | custom-call | flops 8053063680 | bytes 8388608 | tf_op jit(solution)/shard_map/spectra/pallas_call | solution.py:256
  480.3 13.2 %spectra.6.refs_9_ = f32[16,1024,128]{2,1,0:T(8,128)} custom-call(f32[16,4,8,1024]{3,2,1,0:T(8,128)} %all_to_all.26.refs_0_, bf16[16,512,512]{2,1,0:T(8,128)(2,1)} %get-tuple-element.12.refs_1_, bf16[16,512,512]{2,1,0:T(8,128)(2,1)} %get-tuple-element.13.refs_2_, bf16[256,512]{1,0:T(8,128)(2,1)} %constant.25.clone.refs_3_, ...), custom_call_target="tpu_custom_call", output_to_operand_aliasing={{}: (9, {})} | custom-call | flops 8053063680 | bytes 8388608 | tf_op jit(solution)/shard_map/spectra/pallas_call | solution.py:256
  493.5 0.0 all-to-all-done.1.refs_0_
  493.5 1.3 copy-done.1
  494.8 13.2 %spectra.7 = f32[16,1024,128]{2,1,0:T(8,128)} custom-call(f32[16,4,8,1024]{3,2,1,0:T(8,128)} %copy-done.1, bf16[16,512,512]{2,1,0:T(8,128)(2,1)} %get-tuple-element.12.refs_1_, bf16[16,512,512]{2,1,0:T(8,128)(2,1)} %get-tuple-element.13.refs_2_, bf16[256,512]{1,0:T(8,128)(2,1)} %constant.25.clone.refs_3_, ...), custom_call_target="tpu_custom_call", output_to_operand_aliasing={{}: (9, {})} | custom-call | flops 8053063680 | bytes 8388608 | tf_op jit(solution)/shard_map/spectra/pallas_call | solution.py:256
  (13 shorter events, 0.0 us)
Async XLA Ops:
  9.8 194.1 %copy-start.4 = (s32[2,8,256]{2,1,0:T(8,128)S(1)}, s32[2,8,256]{2,1,0:T(8,128)}, u32[]{:S(2)}) copy-start(s32[2,8,256]{2,1,0:T(8,128)} %param.15) | copy-start | bytes 49156
  9.8 194.1 %copy-start.5 = (s32[1,8,256]{2,1,0:T(8,128)S(1)}, s32[1,8,256]{2,1,0:T(8,128)}, u32[]{:S(2)}) copy-start(s32[1,8,256]{2,1,0:T(8,128)} %constant.35) | copy-start | bytes 24580
  9.8 194.1 %copy-start.6 = (s32[1,8,256]{2,1,0:T(8,128)S(1)}, s32[1,8,256]{2,1,0:T(8,128)}, u32[]{:S(2)}) copy-start(s32[1,8,256]{2,1,0:T(8,128)} %constant.34) | copy-start | bytes 24580
  199.1 3.4 copy-start
  202.6 6.9 %collective-permute-start = (f32[256,32]{1,0:T(8,128)S(1)}, f32[256,32]{1,0:T(8,128)S(1)}, u32[]{:S(2)}, u32[]{:S(2)}) collective-permute-start(f32[256,32]{1,0:T(8,128)S(1)} %bitcast.41), channel_id=1, source_target_pairs={{1,0},{2,1},{3,2},{4,3},{5,4},{6,5},{7,6},{8,7},{9,8},{10,9},{11,1... | collective-permute-start | bytes 98312 | tf_op jit(solution)/shard_map/ppermute | solution.py:25
  273.9 110.0 %copy-start.2 = (f32[64,8,1024]{2,1,0:T(8,128)S(1)}, f32[64,8,1024]{2,1,0:T(8,128)}, u32[]{:S(2)}) copy-start(f32[64,8,1024]{2,1,0:T(8,128)} %get-tuple-element.16) | copy-start | bytes 6291460
  273.9 166.6 %copy-start.3 = (f32[2,201,64]{1,2,0:T(8,128)S(1)}, f32[2,201,64]{1,2,0:T(8,128)}, u32[]{:S(2)}) copy-start(f32[2,201,64]{1,2,0:T(8,128)} %param.17) | copy-start | bytes 308740
  273.9 167.7 %copy-start.7 = (s32[1,16,2]{1,2,0:T(2,128)S(1)}, s32[1,16,2]{1,2,0:T(2,128)}, u32[]{:S(2)}) copy-start(s32[1,16,2]{1,2,0:T(2,128)} %param.18) | copy-start | bytes 388
  436.6 56.8 %all-to-all-start.1 = ((f32[16,4,8,1024]{3,2,1,0:T(8,128)}), f32[16,4,8,1024]{3,2,1,0:T(8,128)S(1)}, u32[]{:S(2)}, u32[]{:S(2)}) async-start(f32[16,4,8,1024]{3,2,1,0:T(8,128)} %bitcast.36), calls=%async_computation.1 | async-start | bytes 4194304 | tf_op jit(solution)/shard_map/all_to_all | solution.py:310
  493.5 1.3 copy-start.1

commit v2 on v1

--- a/solution.py
+++ b/solution.py
@@ -33,7 +33,7 @@
     lane = lax.broadcasted_iota(jnp.int32, (SUBS, LANES), 1)
     sub = lax.broadcasted_iota(jnp.int32, (SUBS, LANES), 0)
 
-    @pl.loop(0, rows, unroll=4)
+    @pl.loop(0, rows, unroll=8)
     def _(r):
         head = x_ref[r, :, 0:LANES]
         buf_a[r, :, 0:width] = x_ref[r]
@@ -44,7 +44,7 @@
         a = low_ref[section, r]
         b = high_ref[section, r]
         d = delay_ref[section, r]
-        turn = lax.rem(LANES - d, LANES)
+        turn = (LANES - d) & (LANES - 1)
         keep = lane < LANES - d
         turned = [
             pltpu.roll(src[b, :, i * LANES : (i + 1) * LANES], turn, 1) for i in range(tiles + 1)
@@ -58,14 +58,14 @@
     src, dst = buf_a, buf_b
     for section in range(sections - 1):
 
-        @pl.loop(0, rows, unroll=4)
+        @pl.loop(0, rows, unroll=8)
         def _(r, src=src, dst=dst, section=section):
             merge(src, section, r, dst, r, tiles + 1)
 
         src, dst = dst, src
     for q in range(chunks):
 
-        @pl.loop(0, per, unroll=4)
+        @pl.loop(0, per, unroll=8)
         def _(i, q=q, src=src):
             merge(src, sections - 1, row_ref[q, i], outs[q], i, tiles)
 
@@ -189,7 +189,8 @@
 
 def spectra_kernel(zsel, half_taps, aliased, *refs):
     x_ref, bh_ref, bl_ref, fh, fl, tc, ts, sh, sl = refs[:9]
-    out_ref = refs[10] if aliased else refs[9]
+    out_ref, done_ref = refs[10:] if aliased else refs[9:]
+    done_ref[...] = jnp.zeros_like(done_ref)
     cols = tc.shape[0]
     outs = cols // 2
     x = x_ref[...]
@@ -256,10 +257,16 @@
     return pl.pallas_call(
         functools.partial(spectra_kernel, zsel, taps // 2, aliased),
         grid=(here,),
-        out_shape=jax.ShapeDtypeStruct((trials, rows, LANES), jnp.float32),
+        out_shape=[
+            jax.ShapeDtypeStruct((trials, rows, LANES), jnp.float32),
+            jax.ShapeDtypeStruct((SUBS, LANES), jnp.float32),
+        ],
         in_specs=[x_spec, band_spec, band_spec, *whole]
         + [pl.BlockSpec(memory_space=pl.ANY)] * len(more),
-        out_specs=pl.BlockSpec((1, rows, LANES), lambda t: (first_trial + t, 0, 0)),
+        out_specs=[
+            pl.BlockSpec((1, rows, LANES), lambda t: (first_trial + t, 0, 0)),
+            pl.BlockSpec((SUBS, LANES), lambda t: (0, 0)),
+        ],
         input_output_aliases={9: 0} if aliased else {},
         compiler_params=pltpu.CompilerParams(vmem_limit_bytes=LIMIT),
         cost_estimate=pl.CostEstimate(
@@ -267,6 +274,22 @@
         ),
         name="spectra",
     )(x, band_high, band_low, *consts, *more)
+
+
+def after_kernel(value_ref, done_ref, out_ref):
+    del value_ref, done_ref, out_ref
+
+
+def after(value, done):
+    anywhere = pl.BlockSpec(memory_space=pl.ANY)
+    return pl.pallas_call(
+        after_kernel,
+        out_shape=jax.ShapeDtypeStruct(value.shape, value.dtype),
+        in_specs=[anywhere, anywhere],
+        out_specs=anywhere,
+        input_output_aliases={0: 0},
+        name="after",
+    )(value, done)
 
 
 def on_device(signal, tree_picks, tree_delays, template_bank, template_pick):
@@ -305,10 +328,14 @@
     consts = [jnp.asarray(c) for c in tables(samples, channels, width, taps)]
     out = None
     size = trials // chunks
+    dones = []
     for q, piece in enumerate(pieces):
+        if q >= 2:
+            piece = after(piece, dones[q - 2])
         piece = piece.reshape(everyone, size, SUBS, width)
         piece = lax.all_to_all(piece, ("tm", "band"), split_axis=0, concat_axis=0, tiled=True)
-        out = spectra(piece, band_high, band_low, consts, zsel, taps, trials, q * size, out)
+        out, done = spectra(piece, band_high, band_low, consts, zsel, taps, trials, q * size, out)
+        dones.append(done)
     out = out.reshape(trials, samples // 2 // LANES, zsel, LANES).transpose(0, 2, 1, 3)
     return out.reshape(1, trials, zsel, samples // 2)
 

time: 509 us -> 487 us (0.957)
  blocking collectives: 352 us -> 245 us
  waiting for transfers between devices: 4.93 us -> 99.9 us
  Pallas kernels: 127 us -> 109 us
  starting transfers between devices: 5.19 us -> 13.3 us
    all_to_all x3 -> x1, blocking collectives: 163 us -> 56 us  [on_device(): lax.all_to_all(piece, ('tm', 'band'), split_axis=0, concat_axis=0, tiled=...]
    all_to_all x1 -> x3, waiting for transfers between devices: 0.01 us -> 95 us  [on_device(): lax.all_to_all(piece, ('tm', 'band'), split_axis=0, concat_axis=0, tiled=...]
    pallas_call x1, Pallas kernels: 63.3 us -> 44.6 us  [tree(): pl.pallas_call(functools.partial(tree_kernel, sections, chunks), out_shap...]
    all_to_all x1 -> x3, starting transfers between devices: 3.9 us -> 12 us  [on_device(): lax.all_to_all(piece, ('tm', 'band'), split_axis=0, concat_axis=0, tiled=...]
  transfers between devices with their start and end apart: 2 -> 4, of which waited for: 1 -> 4; matrix products, arithmetic and copies ran while one was open for 1% -> 1% of each run, Pallas kernels for 10% -> 10%
where the time goes in v2:
time: 487 us; the launch traced here: 486 us
  blocking collectives  245 us (50%)
  Pallas kernels  109 us (22%)
  waiting for transfers between devices  99.9 us (21%)
  local copies, waits for them, and re-layouts  17.4 us (4%)
  starting transfers between devices  13.3 us (3%)
    all_to_all x1, blocking collectives, on_device(): x = lax.all_to_all(folded, 'band', split_axis=0, concat_axis=0, tiled=True)  189 us
    all_to_all x3, waiting for transfers between devices, on_device(): lax.all_to_all(piece, ('tm', 'band'), split_axis=0, concat_axis=0, tiled=...  95 us
    all_to_all x1, blocking collectives, on_device(): lax.all_to_all(piece, ('tm', 'band'), split_axis=0, concat_axis=0, tiled=...  56 us
    pallas_call x4, Pallas kernels, spectra(): pl.pallas_call(functools.partial(spectra_kernel, zsel, taps // 2, aliased...  52.8 us
    pallas_call x1, Pallas kernels, tree(): pl.pallas_call(functools.partial(tree_kernel, sections, chunks), out_shap...  44.6 us
    unnamed x18, local copies, waits for them, and re-layouts  13 us
    all_to_all x3, starting transfers between devices, on_device(): lax.all_to_all(piece, ('tm', 'band'), split_axis=0, concat_axis=0, tiled=...  12 us
    pallas_call x1, Pallas kernels, bands(): pl.pallas_call(functools.partial(bands_kernel, zsel), grid=(trials,), out...  11.3 us
  transfers between devices with their start and end apart: 4, of which 4 were waited for; matrix products, arithmetic and copies ran while one was open for 1% of the time, Pallas kernels for 10%

profile of v2, /device:TPU:0, one launch (start us, length us, event | category | flops | bytes accessed | tf_op | source)
XLA Modules:
  0.0 485.8 jit_solution(6175699757141099988)
XLA Ops:
  0.0 8.1 %copy.28 = f32[8,8,32,1024]{3,2,1,0:T(8,128)S(1)} copy(f32[8,8,32,1024]{3,1,2,0:T(8,128)} %bitcast.37) | data formatting | bytes 16777216
  8.1 1.7 copy.30
  9.8 0.0 copy-start.4
  9.8 0.0 copy-start.5
  9.8 0.0 copy-start.6
  9.8 189.3 %all_to_all.25 = f32[4,64,8,1024]{3,2,1,0:T(8,128)S(1)} all-to-all(f32[4,64,8,1024]{3,2,1,0:T(8,128)S(1)} %bitcast.33), channel_id=1, replica_groups=mesh['beams'=2,'tm'=4,'band'=4] {'band'}, dimensions={0} | all-to-all | bytes 16777216 | tf_op jit(solution)/shard_map/all_to_all | solution.py:313
  199.1 3.4 copy-done
  202.5 0.1 slice.20
  202.6 1.3 collective-permute-start
  204.0 0.6 add_bitcast_fusion
  204.6 4.9 %collective-permute-done = f32[256,32]{1,0:T(8,128)S(1)} collective-permute-done((f32[256,32]{1,0:T(8,128)S(1)}, f32[256,32]{1,0:T(8,128)S(1)}, u32[]{:S(2)}, u32[]{:S(2)}) %collective-permute-start) | collective-permute-done | bytes 32800 | tf_op jit(solution)/shard_map/ppermute | solution.py:25
  209.5 1.0 broadcast_in_dim.4.rim_ref
  210.5 44.6 %tree.1 = (f32[64,8,1024]{2,1,0:T(8,128)}, f32[64,8,1024]{2,1,0:T(8,128)}, f32[64,8,1024]{2,1,0:T(8,128)}, f32[64,8,1024]{2,1,0:T(8,128)}) custom-call(s32[8,256]{1,0:T(8,128)} %get-tuple-element.30.low_ref, s32[8,256]{1,0:T(8,128)} %get-tuple-element.29.high_ref, s32[8,256]{1,0:T(8,128)} %delay_ref.1, s32[4,64]{1,0:T(4,128)} %constant.24.clone.row_ref, ...), custom_call_target="tpu_custom_call" | custom-call | flops 67108864 | bytes 16777216 | tf_op jit(solution)/shard_map/tree/pallas_call | solution.py:79
  255.1 56.0 %all_to_all.26.refs_0_ = f32[16,4,8,1024]{3,2,1,0:T(8,128)} all-to-all(f32[16,4,8,1024]{3,2,1,0:T(8,128)} %bitcast.39), channel_id=1, replica_groups=mesh['beams'=2,'tm'=4,'band'=4] {'tm','band'}, dimensions={0} | all-to-all | bytes 4194304 | tf_op jit(solution)/shard_map/all_to_all | solution.py:336
  311.1 3.7 all-to-all-start.1
  314.9 0.1 copy.27
  315.0 0.7 rev.3
  315.7 0.1 copy.22
  315.8 0.1 pad.6.clone
  315.9 0.3 fusion
  316.3 0.7 copy.26.u_ref
  316.9 11.3 %bands.1 = (bf16[16,512,512]{2,1,0:T(8,128)(2,1)}, bf16[16,512,512]{2,1,0:T(8,128)(2,1)}) custom-call(f32[16,4,256]{2,1,0:T(4,128)} %copy.26.u_ref), custom_call_target="tpu_custom_call" | custom-call | flops 20971520 | bytes 16777216 | tf_op jit(solution)/shard_map/bands/pallas_call | solution.py:138
  328.2 13.2 %spectra.4 = (f32[16,1024,128]{2,1,0:T(8,128)}, f32[8,128]{1,0:T(8,128)}) custom-call(f32[16,4,8,1024]{3,2,1,0:T(8,128)} %all_to_all.26.refs_0_, bf16[16,512,512]{2,1,0:T(8,128)(2,1)} %get-tuple-element.19.refs_1_, bf16[16,512,512]{2,1,0:T(8,128)(2,1)} %get-tuple-element.20.refs_2_, bf16[256,512]{1,0:T(8,128)(2,1)} %constant.25.clone.refs_3_, ...), custom_call_target="tpu_custom_call" | custom-call | flops 8053063680 | bytes 8388608 | tf_op jit(solution)/shard_map/spectra/pallas_call | solution.py:257
  341.4 22.8 %all-to-all-done.1.refs_0_ = f32[16,4,8,1024]{3,2,1,0:T(8,128)S(1)} async-done(((f32[16,4,8,1024]{3,2,1,0:T(8,128)}), f32[16,4,8,1024]{3,2,1,0:T(8,128)S(1)}, u32[]{:S(2)}, u32[]{:S(2)}) %all-to-all-start.1) | async-done | bytes 2097184 | tf_op jit(solution)/shard_map/all_to_all | solution.py:336
  364.2 4.6 all-to-all-start.4
  368.9 13.2 %spectra.5 = (f32[16,1024,128]{2,1,0:T(8,128)}, f32[8,128]{1,0:T(8,128)}) custom-call(f32[16,4,8,1024]{3,2,1,0:T(8,128)} %copy-done.1, bf16[16,512,512]{2,1,0:T(8,128)(2,1)} %get-tuple-element.19.refs_1_, bf16[16,512,512]{2,1,0:T(8,128)(2,1)} %get-tuple-element.20.refs_2_, bf16[256,512]{1,0:T(8,128)(2,1)} %constant.25.clone.refs_3_, ...), custom_call_target="tpu_custom_call", output_to_operand_aliasing={{0}: (9, {})} | custom-call | flops 8053063680 | bytes 8388608 | tf_op jit(solution)/shard_map/spectra/pallas_call | solution.py:257
  382.1 36.0 %all-to-all-done.4.refs_0_ = f32[16,4,8,1024]{3,2,1,0:T(8,128)} async-done(((f32[16,4,8,1024]{3,2,1,0:T(8,128)}), f32[16,4,8,1024]{3,2,1,0:T(8,128)}, u32[]{:S(2)}, u32[]{:S(2)}) %all-to-all-start.4) | async-done | bytes 2097184 | tf_op jit(solution)/shard_map/all_to_all | solution.py:336
  418.1 3.7 all-to-all-start.3
  421.8 13.2 %spectra.6 = (f32[16,1024,128]{2,1,0:T(8,128)}, f32[8,128]{1,0:T(8,128)}) custom-call(f32[16,4,8,1024]{3,2,1,0:T(8,128)} %all-to-all-done.4.refs_0_, bf16[16,512,512]{2,1,0:T(8,128)(2,1)} %get-tuple-element.19.refs_1_, bf16[16,512,512]{2,1,0:T(8,128)(2,1)} %get-tuple-element.20.refs_2_, ...), custom_call_target="tpu_custom_call", output_to_operand_aliasing={{0}: (9, {})} | custom-call | flops 8053063680 | bytes 8388608 | tf_op jit(solution)/shard_map/spectra/pallas_call | solution.py:257
  435.1 36.2 %all-to-all-done.3.refs_0_ = f32[16,4,8,1024]{3,2,1,0:T(8,128)S(1)} async-done(((f32[16,4,8,1024]{3,2,1,0:T(8,128)}), f32[16,4,8,1024]{3,2,1,0:T(8,128)S(1)}, u32[]{:S(2)}, u32[]{:S(2)}) %all-to-all-start.3) | async-done | bytes 2097184 | tf_op jit(solution)/shard_map/all_to_all | solution.py:336
  471.2 1.3 copy-done.2
  472.6 13.2 %spectra.7 = (f32[16,1024,128]{2,1,0:T(8,128)}, f32[8,128]{1,0:T(8,128)}) custom-call(f32[16,4,8,1024]{3,2,1,0:T(8,128)} %copy-done.2, bf16[16,512,512]{2,1,0:T(8,128)(2,1)} %get-tuple-element.19.refs_1_, bf16[16,512,512]{2,1,0:T(8,128)(2,1)} %get-tuple-element.20.refs_2_, bf16[256,512]{1,0:T(8,128)(2,1)} %constant.25.clone.refs_3_, ...), custom_call_target="tpu_custom_call", output_to_operand_aliasing={{0}: (9, {})} | custom-call | flops 8053063680 | bytes 8388608 | tf_op jit(solution)/shard_map/spectra/pallas_call | solution.py:257
  (17 shorter events, 0.1 us)
Async XLA Ops:
  9.8 194.1 %copy-start.4 = (s32[2,8,256]{2,1,0:T(8,128)S(1)}, s32[2,8,256]{2,1,0:T(8,128)}, u32[]{:S(2)}) copy-start(s32[2,8,256]{2,1,0:T(8,128)} %param.15) | copy-start | bytes 49156
  9.8 194.1 %copy-start.5 = (s32[1,8,256]{2,1,0:T(8,128)S(1)}, s32[1,8,256]{2,1,0:T(8,128)}, u32[]{:S(2)}) copy-start(s32[1,8,256]{2,1,0:T(8,128)} %constant.35) | copy-start | bytes 24580
  9.8 194.1 %copy-start.6 = (s32[1,8,256]{2,1,0:T(8,128)S(1)}, s32[1,8,256]{2,1,0:T(8,128)}, u32[]{:S(2)}) copy-start(s32[1,8,256]{2,1,0:T(8,128)} %constant.34) | copy-start | bytes 24580
  199.1 3.4 copy-start
  202.6 6.9 %collective-permute-start = (f32[256,32]{1,0:T(8,128)S(1)}, f32[256,32]{1,0:T(8,128)S(1)}, u32[]{:S(2)}, u32[]{:S(2)}) collective-permute-start(f32[256,32]{1,0:T(8,128)S(1)} %bitcast.41), channel_id=1, source_target_pairs={{1,0},{2,1},{3,2},{4,3},{5,4},{6,5},{7,6},{8,7},{9,8},{10,9},{11,1... | collective-permute-start | bytes 98312 | tf_op jit(solution)/shard_map/ppermute | solution.py:25
  210.5 104.3 %copy-start.3 = (f32[2,201,64]{1,2,0:T(8,128)S(1)}, f32[2,201,64]{1,2,0:T(8,128)}, u32[]{:S(2)}) copy-start(f32[2,201,64]{1,2,0:T(8,128)} %param.17) | copy-start | bytes 308740
  210.5 105.4 %copy-start.7 = (s32[1,16,2]{1,2,0:T(2,128)S(1)}, s32[1,16,2]{1,2,0:T(2,128)}, u32[]{:S(2)}) copy-start(s32[1,16,2]{1,2,0:T(2,128)} %param.18) | copy-start | bytes 388
  311.1 53.1 %all-to-all-start.1 = ((f32[16,4,8,1024]{3,2,1,0:T(8,128)}), f32[16,4,8,1024]{3,2,1,0:T(8,128)S(1)}, u32[]{:S(2)}, u32[]{:S(2)}) async-start(f32[16,4,8,1024]{3,2,1,0:T(8,128)} %bitcast.38), calls=%async_computation.1 | async-start | bytes 4194304 | tf_op jit(solution)/shard_map/all_to_all | solution.py:336
  364.2 4.6 copy-start.1
  364.2 53.9 %all-to-all-start.4 = ((f32[16,4,8,1024]{3,2,1,0:T(8,128)}), f32[16,4,8,1024]{3,2,1,0:T(8,128)}, u32[]{:S(2)}, u32[]{:S(2)}) async-start(f32[16,4,8,1024]{3,2,1,0:T(8,128)} %bitcast.36), calls=%async_computation.4 | async-start | bytes 4194304 | tf_op jit(solution)/shard_map/all_to_all | solution.py:336
  418.1 53.1 %all-to-all-start.3 = ((f32[16,4,8,1024]{3,2,1,0:T(8,128)}), f32[16,4,8,1024]{3,2,1,0:T(8,128)S(1)}, u32[]{:S(2)}, u32[]{:S(2)}) async-start(f32[16,4,8,1024]{3,2,1,0:T(8,128)} %bitcast.35), calls=%async_computation.3 | async-start | bytes 4194304 | tf_op jit(solution)/shard_map/all_to_all | solution.py:336
  471.2 1.3 copy-start.2

commit v3 on v2

--- a/solution.py
+++ b/solution.py
@@ -25,20 +25,28 @@
     return lax.ppermute(value, axis, [(source, source + steps) for source in range(first, last)])
 
 
-def tree_kernel(sections, chunks, low_ref, high_ref, delay_ref, row_ref, x_ref, rim_ref, *rest):
-    outs, (buf_a, buf_b) = rest[:chunks], rest[chunks:]
-    rows, _, width = x_ref.shape
-    tiles = width // LANES
-    per = rows // chunks
+def tree_kernel(sections, sizes, parts, has_rim, *refs):
+    low_ref, high_ref, delay_ref, row_ref = refs[:4]
+    xs, refs = refs[4 : 4 + len(parts)], refs[4 + len(parts) :]
+    if has_rim:
+        rim_ref, refs = refs[0], refs[1:]
+    buf_a, buf_b = refs[-2:]
+    outs = refs[len(refs) - 2 - len(sizes) : -2]
+    rows, _, span = buf_a.shape
+    tiles = span // LANES - 1
     lane = lax.broadcasted_iota(jnp.int32, (SUBS, LANES), 1)
     sub = lax.broadcasted_iota(jnp.int32, (SUBS, LANES), 0)
 
-    @pl.loop(0, rows, unroll=8)
+    @pl.loop(0, rows, unroll=4)
     def _(r):
-        head = x_ref[r, :, 0:LANES]
-        buf_a[r, :, 0:width] = x_ref[r]
-        up = pltpu.roll(head, SUBS - 1, 0)
-        buf_a[r, :, width : width + LANES] = jnp.where(sub == SUBS - 1, rim_ref[r], up)
+        at = 0
+        for x_ref, first in zip(xs, parts):
+            count = x_ref.shape[2] - first
+            buf_a[r, :, at : at + count] = x_ref[r, :, first:]
+            at += count
+        if has_rim:
+            up = pltpu.roll(xs[0][r, :, 0:LANES], SUBS - 1, 0)
+            buf_a[r, :, at : at + LANES] = jnp.where(sub == SUBS - 1, rim_ref[r], up)
 
     def merge(src, section, r, dst, at, count):
         a = low_ref[section, r]
@@ -63,33 +71,42 @@
             merge(src, section, r, dst, r, tiles + 1)
 
         src, dst = dst, src
-    for q in range(chunks):
-
-        @pl.loop(0, per, unroll=8)
-        def _(i, q=q, src=src):
-            merge(src, sections - 1, row_ref[q, i], outs[q], i, tiles)
-
-
-def tree(x, rim, low, high, delays, order):
-    rows, _, width = x.shape
-    chunks, per = order.shape
-    sections = low.shape[0]
+    start = 0
+    for size, out in zip(sizes, outs):
+
+        @pl.loop(0, size, unroll=8)
+        def _(i, start=start, src=src, out=out):
+            merge(src, sections - 1, row_ref[start + i], out, i, tiles)
+
+        start += size
+
+
+def tree(xs, parts, rim, tables_of, sizes, width, span, place, so_far):
+    rows = xs[0].shape[0]
+    sections = tables_of[0].shape[0]
     smem = pl.BlockSpec(memory_space=pltpu.SMEM)
     vmem = pl.BlockSpec(memory_space=pltpu.VMEM)
+    has_rim = rim is not None
+    inputs = [*tables_of, *xs] + ([rim] if has_rim else [])
+    known = len(inputs)
     return pl.pallas_call(
-        functools.partial(tree_kernel, sections, chunks),
-        out_shape=[jax.ShapeDtypeStruct((per, SUBS, width), jnp.float32)] * chunks,
-        in_specs=[smem] * 4 + [vmem] * 2,
-        out_specs=[vmem] * chunks,
-        scratch_shapes=[pltpu.VMEM((rows, SUBS, width + LANES), jnp.float32)] * 2,
+        functools.partial(tree_kernel, sections, sizes, parts, has_rim),
+        grid=(1,),
+        out_shape=[jax.ShapeDtypeStruct((size, SUBS, width), jnp.float32) for size in sizes],
+        in_specs=[smem] * 4
+        + [vmem] * (known - 4)
+        + [pl.BlockSpec(memory_space=pl.ANY)] * len(so_far),
+        out_specs=[pl.BlockSpec((size, SUBS, span), lambda i: (0, 0, place)) for size in sizes],
+        input_output_aliases={known + i: i for i in range(len(so_far))},
+        scratch_shapes=[pltpu.VMEM((rows, SUBS, span + LANES), jnp.float32)] * 2,
         compiler_params=pltpu.CompilerParams(vmem_limit_bytes=LIMIT),
         cost_estimate=pl.CostEstimate(
-            flops=rows * SUBS * width * sections * 4,
-            bytes_accessed=rows * SUBS * width * 8,
+            flops=rows * SUBS * span * sections * 4,
+            bytes_accessed=rows * SUBS * span * 8,
             transcendentals=0,
         ),
         name="tree",
-    )(low, high, delays, order, x, rim)
+    )(*inputs, *so_far)
 
 
 def split(value):
@@ -303,39 +320,60 @@
     slab = signal.shape[1] // band_count
     width = slab // SUBS
     trials = CH_DEV // time_count
-    chunks = min(4, trials)
+    last = max(1, trials // 4)
+    counts = [count for count in (trials - last, last) if count]
     zsel = template_pick.shape[2]
     taps = template_bank.shape[2]
 
     band_high, band_low = bands(template_pick[0], template_bank)
-
-    folded = signal.reshape(CH_DEV, band_count, SUBS, width).transpose(1, 0, 2, 3)
-    x = lax.all_to_all(folded, "band", split_axis=0, concat_axis=0, tiled=True)
-    x = x.reshape(channels, SUBS, width)
-    rim = shifted(x[:, 0, :rim_depth], ("tm", "band"), -1)
-    rim = jnp.pad(rim, ((0, 0), (0, LANES - rim_depth)))
-    rim = jnp.broadcast_to(rim[:, None, :], (channels, SUBS, LANES))
 
     half = (1 << np.arange(sections))[:, None]
     r = np.arange(channels)[None, :]
     base = r - r % (2 * half) + r % half - r % np.minimum(half, CH_DEV)
     low = tree_picks[0] + base.astype(np.int32)
     high = tree_picks[1] + (base + half).astype(np.int32)
-    order = np.arange(channels).reshape(band_count, time_count, chunks, trials // chunks)
-    order = order.transpose(2, 1, 0, 3).reshape(chunks, -1).astype(np.int32)
-    pieces = tree(x, rim, low, high, tree_delays, jnp.asarray(order))
+    grid = np.arange(channels).reshape(band_count, time_count, trials).transpose(1, 0, 2)
+    firsts = [sum(counts[:q]) for q in range(len(counts))]
+    order = np.concatenate(
+        [grid[:, :, first : first + count].reshape(-1) for first, count in zip(firsts, counts)]
+    ).astype(np.int32)
+    tables_of = (low, high, tree_delays, jnp.asarray(order))
+    sizes = [everyone * count for count in counts]
+
+    folded = signal.reshape(CH_DEV, band_count, SUBS, width)
+
+    def exchanged(value):
+        value = lax.all_to_all(value, "band", split_axis=0, concat_axis=0, tiled=True)
+        return value.reshape(channels, SUBS, -1)
+
+    def rim_of(x):
+        rim = shifted(x[:, 0, :rim_depth], ("tm", "band"), -1)
+        rim = jnp.pad(rim, ((0, 0), (0, LANES - rim_depth)))
+        return jnp.broadcast_to(rim[:, None, :], (channels, SUBS, LANES))
+
+    if width % (2 * LANES) == 0:
+        span = width // 2
+        cut = span + LANES
+        x_a = exchanged(folded[..., :cut].transpose(1, 0, 2, 3))
+        x_b = exchanged(after(folded[..., cut:].transpose(1, 0, 2, 3), x_a))
+        pieces = tree([x_a], [0], None, tables_of, sizes, width, span, 0, [])
+        pieces = tree(
+            [x_a, x_b], [span, 0], rim_of(x_a), tables_of, sizes, width, span, 1, pieces
+        )
+    else:
+        x = exchanged(folded.transpose(1, 0, 2, 3))
+        pieces = tree([x], [0], rim_of(x), tables_of, sizes, width, width, 0, [])
 
     consts = [jnp.asarray(c) for c in tables(samples, channels, width, taps)]
     out = None
-    size = trials // chunks
-    dones = []
-    for q, piece in enumerate(pieces):
-        if q >= 2:
-            piece = after(piece, dones[q - 2])
-        piece = piece.reshape(everyone, size, SUBS, width)
-        piece = lax.all_to_all(piece, ("tm", "band"), split_axis=0, concat_axis=0, tiled=True)
-        out, done = spectra(piece, band_high, band_low, consts, zsel, taps, trials, q * size, out)
-        dones.append(done)
+    for first, count, piece in zip(firsts, counts, pieces):
+        piece = piece.reshape(everyone, count, SUBS, width)
+        if out is not None:
+            piece = after(piece, arrived)
+        arrived = lax.all_to_all(piece, ("tm", "band"), split_axis=0, concat_axis=0, tiled=True)
+        out, _ = spectra(
+            arrived, band_high, band_low, consts, zsel, taps, trials, first, out
+        )
     out = out.reshape(trials, samples // 2 // LANES, zsel, LANES).transpose(0, 2, 1, 3)
     return out.reshape(1, trials, zsel, samples // 2)
 

time: 487 us -> 463 us (0.951)
  blocking collectives: 245 us -> 145 us
  waiting for transfers between devices: 99.9 us -> 149 us
  Pallas kernels: 109 us -> 126 us
  local copies, waits for them, and re-layouts: 17.4 us -> 24.4 us
    all_to_all x1 -> x0, blocking collectives: 189 us -> none  [on_device(): x = lax.all_to_all(folded, 'band', split_axis=0, concat_axis=0, tiled=True)]
    all_to_all x0 -> x2, waiting for transfers between devices: none -> 144 us  [exchanged(): lax.all_to_all(value, 'band', split_axis=0, concat_axis=0, tiled=True)]
    all_to_all x3 -> x1, waiting for transfers between devices: 95 us -> 2.36 us  [on_device(): lax.all_to_all(piece, ('tm', 'band'), split_axis=0, concat_axis=0, tiled=...]
    all_to_all x1, blocking collectives: 56 us -> 145 us  [on_device(): lax.all_to_all(piece, ('tm', 'band'), split_axis=0, concat_axis=0, tiled=...]
    pallas_call x1 -> x2, Pallas kernels: 44.6 us -> 68.6 us  [tree(): pl.pallas_call(functools.partial(tree_kernel, sections, sizes, parts, has...]
    all_to_all x0 -> x2, starting transfers between devices: none -> 10.2 us  [exchanged(): lax.all_to_all(value, 'band', split_axis=0, concat_axis=0, tiled=True)]
    all_to_all x3 -> x1, starting transfers between devices: 12 us -> 4.03 us  [on_device(): lax.all_to_all(piece, ('tm', 'band'), split_axis=0, concat_axis=0, tiled=...]
    transpose x0 -> x3, local copies, waits for them, and re-layouts: none -> 7.19 us  [the longest x1 3.87 us: on_device(): x_b = exchanged(after(folded[..., cut:].transpose(1, 0, 2, 3), x_a))]
  transfers between devices with their start and end apart: 4 -> 4, of which waited for: 4 -> 4; matrix products, arithmetic and copies ran while one was open for 1% -> 2% of each run, Pallas kernels for 10% -> 17%
where the time goes in v3:
time: 463 us; the launch traced here: 461 us
  waiting for transfers between devices  149 us (32%)
  blocking collectives  145 us (31%)
  Pallas kernels  126 us (27%)
  local copies, waits for them, and re-layouts  24.4 us (5%)
  starting transfers between devices  15.5 us (3%)
    all_to_all x1, blocking collectives, on_device(): lax.all_to_all(piece, ('tm', 'band'), split_axis=0, concat_axis=0, tiled=...  145 us
    all_to_all x2, waiting for transfers between devices, exchanged(): lax.all_to_all(value, 'band', split_axis=0, concat_axis=0, tiled=True)  144 us
    pallas_call x2, Pallas kernels, tree(): pl.pallas_call(functools.partial(tree_kernel, sections, sizes, parts, has...  68.6 us
    pallas_call x2, Pallas kernels, spectra(): pl.pallas_call(functools.partial(spectra_kernel, zsel, taps // 2, aliased...  46.6 us
    unnamed x18, local copies, waits for them, and re-layouts  13.1 us
    pallas_call x1, Pallas kernels, bands(): pl.pallas_call(functools.partial(bands_kernel, zsel), grid=(trials,), out...  11.3 us
    all_to_all x2, starting transfers between devices, exchanged(): lax.all_to_all(value, 'band', split_axis=0, concat_axis=0, tiled=True)  10.2 us
  transfers between devices with their start and end apart: 4, of which 4 were waited for; matrix products, arithmetic and copies ran while one was open for 2% of the time, Pallas kernels for 17%

profile of v3, /device:TPU:0, one launch (start us, length us, event | category | flops | bytes accessed | tf_op | source)
XLA Modules:
  0.0 461.5 jit_solution(16929331859217456569)
XLA Ops:
  0.0 8.1 %copy.40 = f32[8,8,32,1024]{3,2,1,0:T(8,128)S(1)} copy(f32[8,8,32,1024]{3,1,2,0:T(8,128)} %bitcast.36) | data formatting | bytes 16777216
  8.1 0.0 copy-start
  8.1 0.6 slice_bitcast_fusion
  8.8 2.7 copy-done
  11.5 2.7 copy.30
  14.2 6.3 %all-to-all-start = ((f32[4,64,8,640]{3,2,1,0:T(8,128)}), f32[4,64,8,640]{3,2,1,0:T(8,128)}, u32[]{:S(2)}, u32[]{:S(2)}) async-start(f32[4,64,8,640]{3,2,1,0:T(8,128)} %copy.30), calls=%async_computation | async-start | bytes 10485760 | tf_op jit(solution)/shard_map/all_to_all | solution.py:346
  20.5 3.9 copy_bitcast_fusion.value_ref
  24.4 112.2 %all-to-all-done = f32[4,64,8,640]{3,2,1,0:T(8,128)} async-done(((f32[4,64,8,640]{3,2,1,0:T(8,128)}), f32[4,64,8,640]{3,2,1,0:T(8,128)}, u32[]{:S(2)}, u32[]{:S(2)}) %all-to-all-start) | async-done | bytes 5242912 | tf_op jit(solution)/shard_map/all_to_all | solution.py:346
  136.6 3.8 all-to-all-start.1
  140.5 1.3 slice.30
  141.8 1.3 collective-permute-start
  143.1 0.0 copy-done.4
  143.1 0.6 add_bitcast_fusion
  143.7 33.6 %tree.2 = (f32[192,8,1024]{2,1,0:T(8,128)}, f32[64,8,1024]{2,1,0:T(8,128)}) custom-call(s32[8,256]{1,0:T(8,128)} %get-tuple-element.22.refs_0_, s32[8,256]{1,0:T(8,128)} %get-tuple-element.21.refs_1_, s32[8,256]{1,0:T(8,128)} %refs_2_.3, s32[256]{0:T(256)} %constant.24.clone.refs_3_, f32[256,8,640]{2,1,0:T(8,128)} %bitcast.3.done_ref.refs_4_), custom_call_target="tpu_custom_call" | custom-call | flops 33554432 | bytes 8388608 | tf_op jit(solution)/shard_map/tree/pallas_call | solution.py:92
  177.3 2.5 collective-permute-done
  179.9 31.8 %all-to-all-done.1 = f32[4,64,8,384]{3,2,1,0:T(8,128)S(1)} async-done(((f32[4,64,8,384]{3,2,1,0:T(8,128)}), f32[4,64,8,384]{3,2,1,0:T(8,128)S(1)}, u32[]{:S(2)}, u32[]{:S(2)}) %all-to-all-start.1) | async-done | bytes 3145760 | tf_op jit(solution)/shard_map/all_to_all | solution.py:346
  211.7 1.2 broadcast_in_dim.4.refs_6_
  212.9 0.8 copy-done.1
  213.7 34.9 %tree.3 = (f32[192,8,1024]{2,1,0:T(8,128)}, f32[64,8,1024]{2,1,0:T(8,128)}) custom-call(s32[8,256]{1,0:T(8,128)} %get-tuple-element.22.refs_0_, s32[8,256]{1,0:T(8,128)} %get-tuple-element.21.refs_1_, s32[8,256]{1,0:T(8,128)} %refs_2_.3, s32[256]{0:T(256)} %constant.24.clone.refs_3_, ...), custom_call_target="tpu_custom_call", output_to_operand_aliasing={{0}: (7, {}), {1}: (8, {})} | custom-call | flops 33554432 | bytes 8388608 | tf_op jit(solution)/shard_map/tree/pallas_call | solution.py:92
  248.6 145.1 %all_to_all.20.done_ref.refs_0_ = f32[16,12,8,1024]{3,2,1,0:T(8,128)} all-to-all(f32[16,12,8,1024]{3,2,1,0:T(8,128)} %bitcast.33), channel_id=1, replica_groups=mesh['beams'=2,'tm'=4,'band'=4] {'tm','band'}, dimensions={0} | all-to-all | bytes 12582912 | tf_op jit(solution)/shard_map/all_to_all | solution.py:373
  393.7 4.0 all-to-all-start.3
  397.8 0.1 copy.39
  397.9 0.7 rev.3
  398.6 0.1 copy.33
  398.7 0.1 pad.6.clone
  398.8 0.3 fusion
  399.1 0.7 copy.37.u_ref
  399.8 11.3 %bands.1 = (bf16[16,512,512]{2,1,0:T(8,128)(2,1)}, bf16[16,512,512]{2,1,0:T(8,128)(2,1)}) custom-call(f32[16,4,256]{2,1,0:T(4,128)} %copy.37.u_ref), custom_call_target="tpu_custom_call" | custom-call | flops 20971520 | bytes 16777216 | tf_op jit(solution)/shard_map/bands/pallas_call | solution.py:155
  411.1 33.4 %spectra.2 = (f32[16,1024,128]{2,1,0:T(8,128)}, f32[8,128]{1,0:T(8,128)}) custom-call(f32[16,12,8,1024]{3,2,1,0:T(8,128)} %all_to_all.20.done_ref.refs_0_, bf16[16,512,512]{2,1,0:T(8,128)(2,1)} %get-tuple-element.17.refs_1_, bf16[16,512,512]{2,1,0:T(8,128)(2,1)} %get-tuple-element.18.refs_2_, bf16[256,512]{1,0:T(8,128)(2,1)} %constant.25.clone.refs_3_, ...), custom_call_target="tpu_custom_call" | custom-call | flops 24159191040 | bytes 25165824 | tf_op jit(solution)/shard_map/spectra/pallas_call | solution.py:274
  444.6 2.4 all-to-all-done.3.refs_0_
  446.9 1.3 copy-done.2
  448.3 13.2 %spectra.3 = (f32[16,1024,128]{2,1,0:T(8,128)}, f32[8,128]{1,0:T(8,128)}) custom-call(f32[16,4,8,1024]{3,2,1,0:T(8,128)} %copy-done.2, bf16[16,512,512]{2,1,0:T(8,128)(2,1)} %get-tuple-element.17.refs_1_, bf16[16,512,512]{2,1,0:T(8,128)(2,1)} %get-tuple-element.18.refs_2_, bf16[256,512]{1,0:T(8,128)(2,1)} %constant.25.clone.refs_3_, ...), custom_call_target="tpu_custom_call", output_to_operand_aliasing={{0}: (9, {})} | custom-call | flops 8053063680 | bytes 8388608 | tf_op jit(solution)/shard_map/spectra/pallas_call | solution.py:274
  (17 shorter events, 0.1 us)
Async XLA Ops:
  8.1 3.4 copy-start
  14.2 122.4 %all-to-all-start = ((f32[4,64,8,640]{3,2,1,0:T(8,128)}), f32[4,64,8,640]{3,2,1,0:T(8,128)}, u32[]{:S(2)}, u32[]{:S(2)}) async-start(f32[4,64,8,640]{3,2,1,0:T(8,128)} %copy.30), calls=%async_computation | async-start | bytes 10485760 | tf_op jit(solution)/shard_map/all_to_all | solution.py:346
  136.6 6.5 %copy-start.4 = (s32[2,8,256]{2,1,0:T(8,128)S(1)}, s32[2,8,256]{2,1,0:T(8,128)}, u32[]{:S(2)}) copy-start(s32[2,8,256]{2,1,0:T(8,128)} %param.15) | copy-start | bytes 49156
  136.6 6.5 %copy-start.5 = (s32[1,8,256]{2,1,0:T(8,128)S(1)}, s32[1,8,256]{2,1,0:T(8,128)}, u32[]{:S(2)}) copy-start(s32[1,8,256]{2,1,0:T(8,128)} %constant.35) | copy-start | bytes 24580
  136.6 6.5 %copy-start.6 = (s32[1,8,256]{2,1,0:T(8,128)S(1)}, s32[1,8,256]{2,1,0:T(8,128)}, u32[]{:S(2)}) copy-start(s32[1,8,256]{2,1,0:T(8,128)} %constant.34) | copy-start | bytes 24580
  136.6 75.1 %all-to-all-start.1 = ((f32[4,64,8,384]{3,2,1,0:T(8,128)}), f32[4,64,8,384]{3,2,1,0:T(8,128)S(1)}, u32[]{:S(2)}, u32[]{:S(2)}) async-start(f32[4,64,8,384]{3,2,1,0:T(8,128)} %after.2), calls=%async_computation.1 | async-start | bytes 6291456 | tf_op jit(solution)/shard_map/all_to_all | solution.py:346
  141.8 38.1 %collective-permute-start = (f32[256,32]{1,0:T(8,128)S(1)}, f32[256,32]{1,0:T(8,128)S(1)}, u32[]{:S(2)}, u32[]{:S(2)}) collective-permute-start(f32[256,32]{1,0:T(8,128)S(1)} %bitcast.38), channel_id=1, source_target_pairs={{1,0},{2,1},{3,2},{4,3},{5,4},{6,5},{7,6},{8,7},{9,8},{10,9},{11,1... | collective-permute-start | bytes 98312 | tf_op jit(solution)/shard_map/ppermute | solution.py:25
  211.7 2.0 copy-start.1
  393.7 4.0 copy-start.3
  393.7 5.1 %copy-start.7 = (s32[1,16,2]{1,2,0:T(2,128)S(1)}, s32[1,16,2]{1,2,0:T(2,128)}, u32[]{:S(2)}) copy-start(s32[1,16,2]{1,2,0:T(2,128)} %param.18) | copy-start | bytes 388
  393.7 53.2 %all-to-all-start.3 = ((f32[16,4,8,1024]{3,2,1,0:T(8,128)}), f32[16,4,8,1024]{3,2,1,0:T(8,128)S(1)}, u32[]{:S(2)}, u32[]{:S(2)}) async-start(f32[16,4,8,1024]{3,2,1,0:T(8,128)} %after.3), calls=%async_computation.3 | async-start | bytes 4194304 | tf_op jit(solution)/shard_map/all_to_all | solution.py:373
  446.9 1.3 copy-start.2

commit v4 on v3

--- a/solution.py
+++ b/solution.py
@@ -66,7 +66,7 @@
     src, dst = buf_a, buf_b
     for section in range(sections - 1):
 
-        @pl.loop(0, rows, unroll=8)
+        @pl.loop(0, rows, unroll=16)
         def _(r, src=src, dst=dst, section=section):
             merge(src, section, r, dst, r, tiles + 1)
 
@@ -74,7 +74,7 @@
     start = 0
     for size, out in zip(sizes, outs):
 
-        @pl.loop(0, size, unroll=8)
+        @pl.loop(0, size, unroll=16)
         def _(i, start=start, src=src, out=out):
             merge(src, sections - 1, row_ref[start + i], out, i, tiles)
 
@@ -320,7 +320,7 @@
     slab = signal.shape[1] // band_count
     width = slab // SUBS
     trials = CH_DEV // time_count
-    last = max(1, trials // 4)
+    last = max(1, 3 * trials // 16)
     counts = [count for count in (trials - last, last) if count]
     zsel = template_pick.shape[2]
     taps = template_bank.shape[2]
@@ -355,7 +355,8 @@
         span = width // 2
         cut = span + LANES
         x_a = exchanged(folded[..., :cut].transpose(1, 0, 2, 3))
-        x_b = exchanged(after(folded[..., cut:].transpose(1, 0, 2, 3), x_a))
+        x_b = after(after(folded[..., cut:].transpose(1, 0, 2, 3), x_a), band_low)
+        x_b = exchanged(x_b)
         pieces = tree([x_a], [0], None, tables_of, sizes, width, span, 0, [])
         pieces = tree(
             [x_a, x_b], [span, 0], rim_of(x_a), tables_of, sizes, width, span, 1, pieces

time: 463 us -> 451 us (0.974)
  Pallas kernels: 126 us -> 109 us
  blocking collectives: 145 us -> 156 us
  waiting for transfers between devices: 149 us -> 144 us
    pallas_call x2, Pallas kernels: 68.6 us -> 50.9 us  [tree(): pl.pallas_call(functools.partial(tree_kernel, sections, sizes, parts, has...]
    all_to_all x2, waiting for transfers between devices: 144 us -> 131 us  [exchanged(): lax.all_to_all(value, 'band', split_axis=0, concat_axis=0, tiled=True)]
    all_to_all x1, blocking collectives: 145 us -> 156 us  [on_device(): lax.all_to_all(piece, ('tm', 'band'), split_axis=0, concat_axis=0, tiled=...]
    ppermute x1, waiting for transfers between devices: 2.52 us -> 11.3 us  [shifted(): lax.ppermute(value, axis, [(source, source + steps) for source in range(f...]
  transfers between devices with their start and end apart: 4 -> 4, of which waited for: 4 -> 4; matrix products, arithmetic and copies ran while one was open for 2% -> 2% of each run, Pallas kernels for 17% -> 16%
where the time goes in v4:
time: 451 us; the launch traced here: 450 us
  blocking collectives  156 us (35%)
  waiting for transfers between devices  144 us (32%)
  Pallas kernels  109 us (24%)
  local copies, waits for them, and re-layouts  24.3 us (5%)
  starting transfers between devices  15.5 us (3%)
    all_to_all x1, blocking collectives, on_device(): lax.all_to_all(piece, ('tm', 'band'), split_axis=0, concat_axis=0, tiled=...  156 us
    all_to_all x2, waiting for transfers between devices, exchanged(): lax.all_to_all(value, 'band', split_axis=0, concat_axis=0, tiled=True)  131 us
    pallas_call x2, Pallas kernels, tree(): pl.pallas_call(functools.partial(tree_kernel, sections, sizes, parts, has...  50.9 us
    pallas_call x2, Pallas kernels, spectra(): pl.pallas_call(functools.partial(spectra_kernel, zsel, taps // 2, aliased...  46.6 us
    unnamed x18, local copies, waits for them, and re-layouts  13.1 us
    ppermute x1, waiting for transfers between devices, shifted(): lax.ppermute(value, axis, [(source, source + steps) for source in range(f...  11.3 us
    pallas_call x1, Pallas kernels, bands(): pl.pallas_call(functools.partial(bands_kernel, zsel), grid=(trials,), out...  11.2 us
    all_to_all x2, starting transfers between devices, exchanged(): lax.all_to_all(value, 'band', split_axis=0, concat_axis=0, tiled=True)  10.3 us
  transfers between devices with their start and end apart: 4, of which 4 were waited for; matrix products, arithmetic and copies ran while one was open for 2% of the time, Pallas kernels for 16%

profile of v4, /device:TPU:0, one launch (start us, length us, event | category | flops | bytes accessed | tf_op | source)
XLA Modules:
  0.0 449.9 jit_solution(6023776304432600187)
XLA Ops:
  0.0 8.1 %copy.41 = f32[8,8,32,1024]{3,2,1,0:T(8,128)S(1)} copy(f32[8,8,32,1024]{3,1,2,0:T(8,128)} %bitcast.36) | data formatting | bytes 16777216
  8.1 0.0 copy-start
  8.1 0.6 slice_bitcast_fusion
  8.8 2.7 copy-done
  11.5 2.7 copy.31
  14.2 6.4 %all-to-all-start = ((f32[4,64,8,640]{3,2,1,0:T(8,128)}), f32[4,64,8,640]{3,2,1,0:T(8,128)}, u32[]{:S(2)}, u32[]{:S(2)}) async-start(f32[4,64,8,640]{3,2,1,0:T(8,128)} %copy.31), calls=%async_computation | async-start | bytes 10485760 | tf_op jit(solution)/shard_map/all_to_all | solution.py:346
  20.7 0.0 copy-done.3
  20.7 0.1 copy.40
  20.8 0.7 rev.3
  21.5 0.1 copy.34
  21.6 0.1 pad.6.clone
  21.7 0.3 fusion
  22.1 0.7 copy.38.u_ref
  22.7 11.2 %bands.1 = (bf16[16,512,512]{2,1,0:T(8,128)(2,1)}, bf16[16,512,512]{2,1,0:T(8,128)(2,1)}) custom-call(f32[16,4,256]{2,1,0:T(4,128)} %copy.38.u_ref), custom_call_target="tpu_custom_call" | custom-call | flops 20971520 | bytes 16777216 | tf_op jit(solution)/shard_map/bands/pallas_call | solution.py:155
  34.0 3.9 copy_bitcast_fusion.value_ref
  37.8 98.9 %all-to-all-done = f32[4,64,8,640]{3,2,1,0:T(8,128)} async-done(((f32[4,64,8,640]{3,2,1,0:T(8,128)}), f32[4,64,8,640]{3,2,1,0:T(8,128)}, u32[]{:S(2)}, u32[]{:S(2)}) %all-to-all-start) | async-done | bytes 5242912 | tf_op jit(solution)/shard_map/all_to_all | solution.py:346
  136.8 3.8 all-to-all-start.1
  140.6 1.3 slice.30
  141.9 1.3 collective-permute-start
  143.2 0.6 add_bitcast_fusion
  143.8 24.8 %tree.2 = (f32[208,8,1024]{2,1,0:T(8,128)}, f32[48,8,1024]{2,1,0:T(8,128)}) custom-call(s32[8,256]{1,0:T(8,128)} %get-tuple-element.22.refs_0_, s32[8,256]{1,0:T(8,128)} %get-tuple-element.21.refs_1_, s32[8,256]{1,0:T(8,128)} %refs_2_.3, s32[256]{0:T(256)} %constant.24.clone.refs_3_, f32[256,8,640]{2,1,0:T(8,128)} %bitcast.3.done_ref.refs_4_), custom_call_target="tpu_custom_call" | custom-call | flops 33554432 | bytes 8388608 | tf_op jit(solution)/shard_map/tree/pallas_call | solution.py:92
  168.7 11.3 %collective-permute-done = f32[256,32]{1,0:T(8,128)S(1)} collective-permute-done((f32[256,32]{1,0:T(8,128)S(1)}, f32[256,32]{1,0:T(8,128)S(1)}, u32[]{:S(2)}, u32[]{:S(2)}) %collective-permute-start) | collective-permute-done | bytes 32800 | tf_op jit(solution)/shard_map/ppermute | solution.py:25
  180.0 31.8 %all-to-all-done.1 = f32[4,64,8,384]{3,2,1,0:T(8,128)S(1)} async-done(((f32[4,64,8,384]{3,2,1,0:T(8,128)}), f32[4,64,8,384]{3,2,1,0:T(8,128)S(1)}, u32[]{:S(2)}, u32[]{:S(2)}) %all-to-all-start.1) | async-done | bytes 3145760 | tf_op jit(solution)/shard_map/all_to_all | solution.py:346
  211.8 1.1 broadcast_in_dim.5.refs_6_
  213.0 0.9 copy-done.1
  213.8 26.1 %tree.3 = (f32[208,8,1024]{2,1,0:T(8,128)}, f32[48,8,1024]{2,1,0:T(8,128)}) custom-call(s32[8,256]{1,0:T(8,128)} %get-tuple-element.22.refs_0_, s32[8,256]{1,0:T(8,128)} %get-tuple-element.21.refs_1_, s32[8,256]{1,0:T(8,128)} %refs_2_.3, s32[256]{0:T(256)} %constant.24.clone.refs_3_, ...), custom_call_target="tpu_custom_call", output_to_operand_aliasing={{0}: (7, {}), {1}: (8, {})} | custom-call | flops 33554432 | bytes 8388608 | tf_op jit(solution)/shard_map/tree/pallas_call | solution.py:92
  239.9 156.3 %all_to_all.20.done_ref.refs_0_ = f32[16,13,8,1024]{3,2,1,0:T(8,128)} all-to-all(f32[16,13,8,1024]{3,2,1,0:T(8,128)} %bitcast.33), channel_id=1, replica_groups=mesh['beams'=2,'tm'=4,'band'=4] {'tm','band'}, dimensions={0} | all-to-all | bytes 13631488 | tf_op jit(solution)/shard_map/all_to_all | solution.py:374
  396.2 3.9 all-to-all-start.3
  400.1 35.9 %spectra.2 = (f32[16,1024,128]{2,1,0:T(8,128)}, f32[8,128]{1,0:T(8,128)}) custom-call(f32[16,13,8,1024]{3,2,1,0:T(8,128)} %all_to_all.20.done_ref.refs_0_, bf16[16,512,512]{2,1,0:T(8,128)(2,1)} %get-tuple-element.18.refs_1_, bf16[16,512,512]{2,1,0:T(8,128)(2,1)} %get-tuple-element.13.done_ref.refs_2_, bf16[256,512]{1,0:T(8,128)(2,1)} %constant.25.clone.refs_3_, ...), custom_call_target="tpu_custom_call" | custom-call | flops 26172456960 | bytes 27262976 | tf_op jit(solution)/shard_map/spectra/pallas_call | solution.py:274
  436.1 2.0 all-to-all-done.3.refs_0_
  438.1 1.2 copy-done.2
  439.3 10.7 %spectra.3 = (f32[16,1024,128]{2,1,0:T(8,128)}, f32[8,128]{1,0:T(8,128)}) custom-call(f32[16,3,8,1024]{3,2,1,0:T(8,128)} %copy-done.2, bf16[16,512,512]{2,1,0:T(8,128)(2,1)} %get-tuple-element.18.refs_1_, bf16[16,512,512]{2,1,0:T(8,128)(2,1)} %get-tuple-element.13.done_ref.refs_2_, ...), custom_call_target="tpu_custom_call", output_to_operand_aliasing={{0}: (9, {})} | custom-call | flops 6039797760 | bytes 6291456 | tf_op jit(solution)/shard_map/spectra/pallas_call | solution.py:274
  (18 shorter events, 0.0 us)
Async XLA Ops:
  8.1 3.4 copy-start
  14.2 6.5 %copy-start.3 = (f32[2,201,64]{1,2,0:T(8,128)S(1)}, f32[2,201,64]{1,2,0:T(8,128)}, u32[]{:S(2)}) copy-start(f32[2,201,64]{1,2,0:T(8,128)} %param.17) | copy-start | bytes 308740
  14.2 7.5 %copy-start.7 = (s32[1,16,2]{1,2,0:T(2,128)S(1)}, s32[1,16,2]{1,2,0:T(2,128)}, u32[]{:S(2)}) copy-start(s32[1,16,2]{1,2,0:T(2,128)} %param.18) | copy-start | bytes 388
  14.2 122.5 %all-to-all-start = ((f32[4,64,8,640]{3,2,1,0:T(8,128)}), f32[4,64,8,640]{3,2,1,0:T(8,128)}, u32[]{:S(2)}, u32[]{:S(2)}) async-start(f32[4,64,8,640]{3,2,1,0:T(8,128)} %copy.31), calls=%async_computation | async-start | bytes 10485760 | tf_op jit(solution)/shard_map/all_to_all | solution.py:346
  136.7 6.5 %copy-start.4 = (s32[2,8,256]{2,1,0:T(8,128)S(1)}, s32[2,8,256]{2,1,0:T(8,128)}, u32[]{:S(2)}) copy-start(s32[2,8,256]{2,1,0:T(8,128)} %param.15) | copy-start | bytes 49156
  136.8 6.5 %copy-start.5 = (s32[1,8,256]{2,1,0:T(8,128)S(1)}, s32[1,8,256]{2,1,0:T(8,128)}, u32[]{:S(2)}) copy-start(s32[1,8,256]{2,1,0:T(8,128)} %constant.35) | copy-start | bytes 24580
  136.8 6.5 %copy-start.6 = (s32[1,8,256]{2,1,0:T(8,128)S(1)}, s32[1,8,256]{2,1,0:T(8,128)}, u32[]{:S(2)}) copy-start(s32[1,8,256]{2,1,0:T(8,128)} %constant.34) | copy-start | bytes 24580
  136.8 75.1 %all-to-all-start.1 = ((f32[4,64,8,384]{3,2,1,0:T(8,128)}), f32[4,64,8,384]{3,2,1,0:T(8,128)S(1)}, u32[]{:S(2)}, u32[]{:S(2)}) async-start(f32[4,64,8,384]{3,2,1,0:T(8,128)} %after.4), calls=%async_computation.1 | async-start | bytes 6291456 | tf_op jit(solution)/shard_map/all_to_all | solution.py:346
  141.9 38.1 %collective-permute-start = (f32[256,32]{1,0:T(8,128)S(1)}, f32[256,32]{1,0:T(8,128)S(1)}, u32[]{:S(2)}, u32[]{:S(2)}) collective-permute-start(f32[256,32]{1,0:T(8,128)S(1)} %bitcast.38), channel_id=1, source_target_pairs={{1,0},{2,1},{3,2},{4,3},{5,4},{6,5},{7,6},{8,7},{9,8},{10,9},{11,1... | collective-permute-start | bytes 98312 | tf_op jit(solution)/shard_map/ppermute | solution.py:25
  211.8 2.0 copy-start.1
  396.2 41.9 %all-to-all-start.3 = ((f32[16,3,8,1024]{3,2,1,0:T(8,128)}), f32[16,3,8,1024]{3,2,1,0:T(8,128)S(1)}, u32[]{:S(2)}, u32[]{:S(2)}) async-start(f32[16,3,8,1024]{3,2,1,0:T(8,128)} %after.5), calls=%async_computation.3 | async-start | bytes 3145728 | tf_op jit(solution)/shard_map/all_to_all | solution.py:374
  438.1 1.2 copy-start.2
